TPU v7x, 256 devices: a whole 4x4x8 slice. The times are simulated.
256 devices in a mesh: vel: 32 (over y, x, core), grp: 8 (over z).
Axes of the slice: x: 4, y: 4, z: 8, core: 2. Of those that a mesh axis runs over, the one named last changes fastest.
Arguments:
- adjoint: bfloat16 [512, 8, 32, 2048], P('vel', 'grp'), may hold values from -33 to 33
- relaxation: float32 [8, 32, 2048], P('grp', 'vel'), may hold values from 0.6 to 1.9
- reaction: float32 [8, 32, 2048], P('grp', 'vel'), may hold values from 0.05 to 0.6
- base_moments: float32 [10, 8, 32, 2048], P(None, 'grp', 'vel'), may hold values from -6 to 6
- cell_kind: int32 [8, 32, 2048], P('grp', 'vel'), may hold values from 0 to 2
- patch_id: int32 [8, 32, 2048], P('grp', 'vel'), may hold values from 0 to 4095, as said below
Outputs:
- adjoint_out: bfloat16 [512, 8, 32, 2048], P(None, 'grp', 'vel')
- patch_grad: float32 [4096], P(('vel', 'grp'))
Inputs may be any that keep to these rules, and one draw needn't show every extreme that they name: For a voxel of layer g * 32 + l, (patch_id // 16) % 8 equals g.
All inputs are finite; a program needn't handle non-finite values.
Results may differ from a plain program's by a relative error of at most 0.0036.
Values may be sent and summed in bfloat16 or wider, within the bound.
A program may use at most 128 MiB of HBM per device.

v0:
```python
import jax
import jax.numpy as jnp
from jax import lax
from jax.sharding import PartitionSpec as P

NV = 8
MOMENTS = 10
PY = 16
PZ = 128
PATCH_DEV = 16
Q = 512


courant = 0.3


def with_halo(block, sides, width):
    for axis, dim in sides:
        count = lax.axis_size(axis)
        forward = [(i, i + 1) for i in range(count - 1)]
        backward = [(target, source) for source, target in forward]
        low = lax.ppermute(
            lax.slice_in_dim(block, block.shape[dim] - width, None, axis=dim), axis, forward
        )
        high = lax.ppermute(lax.slice_in_dim(block, 0, width, axis=dim), axis, backward)
        block = jnp.concatenate([low, block, high], axis=dim)
    return block


def component(grid_digit):
    signed = jnp.where(grid_digit % 2 == 0, -1.0, 1.0).astype(jnp.float32)
    return signed * ((grid_digit // 2).astype(jnp.float32) + 0.5) / (NV / 2.0 - 0.5)


def velocities(vel_index):
    return (
        component(vel_index % NV),
        component(vel_index // NV % NV),
        component(vel_index // (NV * NV)),
    )


def moment_basis(vel_x, vel_y, vel_z):
    third_part = 1.0 / 3.0
    return jnp.stack(
        [
            jnp.ones_like(vel_x),
            vel_x,
            vel_y,
            vel_z,
            vel_x * vel_x - third_part,
            vel_y * vel_y - third_part,
            vel_z * vel_z - third_part,
            vel_x * vel_y,
            vel_x * vel_z,
            vel_y * vel_z,
        ]
    )


def advect_block(extended_part, vel_x, vel_y, vel_z):
    row_total, padded_layers, plane_cells = extended_part.shape
    layers = padded_layers - 2
    shape_col = (-1, 1, 1)
    widened = extended_part.astype(jnp.float32)
    centre = widened[:, 1:-1]
    along_x = jnp.where(vel_x.reshape(shape_col) > 0, widened[:, 2:], widened[:, :-2])
    grid_form = centre.reshape(row_total, layers, PY, PZ)
    grid_col = (-1, 1, 1, 1)
    along_y = jnp.where(
        vel_y.reshape(grid_col) > 0, jnp.roll(grid_form, -1, 2), jnp.roll(grid_form, 1, 2)
    ).reshape(row_total, layers, plane_cells)
    along_z = jnp.where(
        vel_z.reshape(grid_col) > 0, jnp.roll(grid_form, -1, 3), jnp.roll(grid_form, 1, 3)
    ).reshape(row_total, layers, plane_cells)
    rate_x = courant * jnp.abs(vel_x).reshape(shape_col)
    rate_y = courant * jnp.abs(vel_y).reshape(shape_col)
    rate_z = courant * jnp.abs(vel_z).reshape(shape_col)
    mixed = (
        (1.0 - rate_x - rate_y - rate_z) * centre
        + rate_x * along_x
        + rate_y * along_y
        + rate_z * along_z
    )
    return mixed.astype(jnp.bfloat16)


def body(adjoint, relaxation, reaction, base_moments, cell_kind, patch_id):
    local_vel, _, layers, plane_cells = adjoint.shape
    vel_count = lax.axis_size("vel")
    grp_count = lax.axis_size("grp")
    flat_input = adjoint.reshape(local_vel, layers, plane_cells)
    extended = with_halo(flat_input, (("grp", 1),), 1)
    own_index = lax.axis_index("vel") * local_vel + jnp.arange(local_vel, dtype=jnp.int32)
    own_x, own_y, own_z = velocities(own_index)
    arrived = lax.all_to_all(
        advect_block(extended, own_x, own_y, own_z), "vel", split_axis=1, concat_axis=0, tiled=True
    )
    space_rows = arrived.reshape(Q, plane_cells)
    vel_index = jnp.arange(Q, dtype=jnp.int32)
    vel_x, vel_y, vel_z = velocities(vel_index)
    poly_basis = moment_basis(vel_x, vel_y, vel_z)
    speed_sq = vel_x * vel_x + vel_y * vel_y + vel_z * vel_z
    weight = jnp.exp(-speed_sq)
    absorb = speed_sq / 3.0
    total_weight = jnp.sum(weight)
    etable = jnp.concatenate([poly_basis * weight, poly_basis * (weight * absorb)], axis=0)
    mu_wide = space_rows.astype(jnp.float32)
    projected = jnp.dot(etable, mu_wide, precision=lax.Precision.HIGHEST)
    kind_flat = cell_kind.reshape(-1)
    is_wall = kind_flat == 2
    fluid_mask = jnp.where(kind_flat != 0, 1.0, 0.0).astype(jnp.float32)
    wall_rate = jnp.where(is_wall, reaction.reshape(-1), 0.0)
    moments = (projected[:MOMENTS] - wall_rate * projected[MOMENTS:]) / total_weight
    relax_rate = relaxation.reshape(-1)
    collided = jnp.dot(poly_basis.T, moments, precision=lax.Precision.HIGHEST)
    damped = (1.0 - wall_rate * absorb[:, None]) * mu_wide
    adjoint_out = (fluid_mask * ((1.0 - relax_rate) * damped + relax_rate * collided)).astype(
        jnp.bfloat16
    )
    sensitivity = (
        -wall_rate
        * jnp.sum(base_moments.reshape(MOMENTS, -1) * projected[MOMENTS:], axis=0)
        / total_weight
    )
    patch_flat = patch_id.reshape(-1)
    owner_block = patch_flat // PATCH_DEV
    group_slot = owner_block // grp_count * PATCH_DEV + patch_flat % PATCH_DEV
    totals = jax.ops.segment_sum(sensitivity, group_slot, num_segments=PATCH_DEV * vel_count)
    patch_grad = lax.psum_scatter(totals, "vel", scatter_dimension=0, tiled=True)
    return (adjoint_out.reshape(Q, 1, 1, plane_cells), patch_grad)


def solution(mesh):
    placed = (
        P("vel", "grp", None, None),
        P("grp", "vel", None),
        P("grp", "vel", None),
        P(None, "grp", "vel", None),
        P("grp", "vel", None),
        P("grp", "vel", None),
    )
    return jax.shard_map(
        body,
        mesh=mesh,
        in_specs=placed,
        out_specs=(P(None, "grp", "vel", None), P(("vel", "grp"))),
        check_vma=False,
    )
```

profile of v0, /device:TPU:1, one launch (start us, length us, event | category | flops | bytes accessed | tf_op | source)
XLA Modules:
  0.0 202.6 jit_solution(7023163646415888201)
XLA Ops:
  0.6 2.7 %copy.15 = bf16[16,1,32,2048]{3,0,2,1:T(8,128)(2,1)S(1)} copy(bf16[16,1,32,2048]{3,2,1,0:T(8,128)(2,1)} %param.6) | data formatting | bytes 4194304 | tf_op args[0]
  3.4 1.3 collective-permute-start.1
  4.7 5.0 %collective-permute-start = (bf16[16,1,2048]{2,0,1:T(8,128)(2,1)S(1)}, bf16[16,1,2048]{2,0,1:T(8,128)(2,1)S(1)}, u32[]{:S(2)}, u32[]{:S(2)}) collective-permute-start(bf16[16,1,2048]{2,0,1:T(8,128)(2,1)S(1)} %get-tuple-element.10), channel_id=1, source_target_pairs={{0,1},{1,2},{2,3},{3,4},{4,5},{5,6},{6,7},{8,9},{9,10},{10,11},{11... | collective-permute-start | bytes 196616 | tf_op jit(solution)/shard_map/ppermute | solution.py:22
  9.9 1.2 collective-permute-done
  11.9 1.5 copy-done
  13.4 0.9 copy.12
  14.3 3.6 %fusion.82 = (f32[16,32,16,1]{3,2,0,1:T(8,128)S(1)}, f32[16,32,16,1]{3,2,0,1:T(8,128)}) fusion(f32[16,32,16,128]{3,2,0,1:T(8,128)S(1)} %bitcast.56), kind=kLoop, calls=%fused_computation.206 | loop fusion | bytes 131072 | tf_op jit(solution)/shard_map/jit(_roll_static)/slice | solution.py:74
  17.9 4.8 %fusion.83 = (f32[16,32,16,127]{3,2,0,1:T(8,128)}, f32[16,32,16,127]{3,2,0,1:T(8,128)}) fusion(f32[16,32,16,128]{3,2,0,1:T(8,128)S(1)} %bitcast.57), kind=kLoop, calls=%fused_computation.207 | loop fusion | bytes 16646144 | tf_op jit(solution)/shard_map/jit(_roll_static)/slice | solution.py:74
  23.1 4.1 %fusion.81 = (f32[16,32,15,128]{3,2,0,1:T(8,128)}, f32[16,32,15,128]{3,2,0,1:T(8,128)}) fusion(f32[16,32,16,128]{3,2,0,1:T(8,128)S(1)} %bitcast.59), kind=kLoop, calls=%fused_computation.205 | loop fusion | bytes 15728640 | tf_op jit(solution)/shard_map/jit(_roll_static)/slice | solution.py:71
  27.1 10.6 %pad_maximum_fusion.2 = (f32[16,32,16,128]{3,2,0,1:T(8,128)}, f32[16,32,16,128]{3,2,0,1:T(8,128)}) fusion(f32[16,32,16,1]{3,2,0,1:T(8,128)} %get-tuple-element.7, f32[16,32,16,127]{3,2,0,1:T(8,128)} %get-tuple-element.9, f32[16,32,16,127]{3,2,0,1:T(8,128)} %get-tuple-element.8, f32[16,32,16,1]{3,2,0,1:T(8,128)S(1)} %get-tuple-element.6), kind=kLoop, calls=%fused_computation.9 | loop fusion | flops 2097152 | bytes 16777216 | tf_op jit(solution)/shard_map/jit(_roll_static)/concatenate | solution.py:74
  37.7 5.0 %concatenate.36 = f32[16,32,2048]{2,0,1:T(8,128)} reshape(f32[16,32,16,128]{3,2,0,1:T(8,128)} %get-tuple-element.24) | data formatting | bytes 8388608 | tf_op jit(solution)/shard_map/jit(_roll_static)/concatenate | solution.py:74
  42.7 4.9 %concatenate.38 = f32[16,32,2048]{2,0,1:T(8,128)} reshape(f32[16,32,16,128]{3,2,0,1:T(8,128)} %get-tuple-element.25) | data formatting | bytes 8388608 | tf_op jit(solution)/shard_map/jit(_roll_static)/concatenate | solution.py:74
  47.6 8.3 %pad_maximum_fusion = (f32[16,32,16,128]{3,2,0,1:T(8,128)}, f32[16,32,16,128]{3,2,0,1:T(8,128)}) fusion(f32[16,32,1,128]{3,2,0,1:T(1,128)S(1)} %get-tuple-element.3, f32[16,32,15,128]{3,2,0,1:T(8,128)} %get-tuple-element.5, f32[16,32,15,128]{3,2,0,1:T(8,128)} %get-tuple-element.4, f32[16,32,1,128]{3,2,0,1:T(1,128)S(1)} %get-tuple-element.2), kind=kLoop, calls=%fused_computation.7 | loop fusion | flops 2097152 | bytes 16777216 | tf_op jit(solution)/shard_map/jit(_roll_static)/concatenate | solution.py:71
  55.9 4.9 %concatenate.32 = f32[16,32,2048]{2,0,1:T(8,128)} reshape(f32[16,32,16,128]{3,2,0,1:T(8,128)} %get-tuple-element.26) | data formatting | bytes 8388608 | tf_op jit(solution)/shard_map/jit(_roll_static)/concatenate | solution.py:71
  60.9 4.9 %concatenate.34 = f32[16,32,2048]{2,0,1:T(8,128)} reshape(f32[16,32,16,128]{3,2,0,1:T(8,128)} %get-tuple-element.27) | data formatting | bytes 8388608 | tf_op jit(solution)/shard_map/jit(_roll_static)/concatenate | solution.py:71
  65.7 12.6 %fusion.4 = bf16[16,32,2048]{2,0,1:T(8,128)(2,1)} fusion(f32[16,34,2048]{2,0,1:T(8,128)} %copy-done, f32[16,32,2048]{2,0,1:T(8,128)} %concatenate.36, f32[16,32,2048]{2,0,1:T(8,128)} %concatenate.38, f32[16,32,2048]{2,0,1:T(8,128)} %concatenate.32, f32[16,32,2048]{2,0,1:T(8,128)} %concatenate.34, f32[16]{0:T(128)S(1)} %get-tuple-element.28, ...), kind=kLoop, calls=%fused_computation.6 | loop fusion | flops 11534336 | bytes 31457584 | tf_op jit(solution)/shard_map/convert_element_type | solution.py:85
  78.4 8.9 %all-to-all-start = ((bf16[16,32,2048]{2,0,1:T(8,128)(2,1)}), bf16[16,32,2048]{2,0,1:T(8,128)(2,1)S(1)}, u32[]{:S(2)}, u32[]{:S(2)}) async-start(bf16[16,32,2048]{2,0,1:T(8,128)(2,1)} %fusion.4), calls=%async_computation | async-start | bytes 4194304 | tf_op jit(solution)/shard_map/all_to_all | solution.py:96
  88.8 0.6 fusion.65
  89.7 25.4 %all-to-all-done = bf16[16,32,2048]{2,0,1:T(8,128)(2,1)S(1)} async-done(((bf16[16,32,2048]{2,0,1:T(8,128)(2,1)}), bf16[16,32,2048]{2,0,1:T(8,128)(2,1)S(1)}, u32[]{:S(2)}, u32[]{:S(2)}) %all-to-all-start) | async-done | bytes 2097184 | tf_op jit(solution)/shard_map/all_to_all | solution.py:96
  115.1 0.9 fusion.13
  116.1 0.6 multiply_divide_fusion
  116.8 14.7 %scatter_custom_fusion = f32[512]{0:T(512)S(1)} fusion(s32[2048]{0:T(1024)S(1)} %bitcast.69, f32[2048]{0:T(1024)S(1)} %multiply_divide_fusion, f32[]{:T(128)} %constant.270.clone.1), kind=kCustom, calls=%fused_computation.173 | custom fusion | flops 2048 | bytes 2052 | tf_op jit(solution)/shard_map/scatter-add | solution.py:129
  131.4 64.4 %all-reduce = f32[512]{0:T(512)S(1)} all-reduce(f32[512]{0:T(512)S(1)} %scatter_custom_fusion), channel_id=2, replica_groups=mesh['vel'=32,'grp'=8] {'vel'}, use_global_device_ids=true, to_apply=%region_3.4.clone | all-reduce | flops 512 | bytes 4096
  196.4 6.2 %fusion.5 = bf16[512,1,1,2048]{3,0,2,1:T(8,128)(2,1)} fusion(f32[10,512]{1,0:T(8,128)S(1)} %stack.2, bf16[512,2048]{1,0:T(8,128)(2,1)S(1)} %bitcast.64, f32[2048]{0:T(1024)S(1)} %bitcast.68, f32[512]{0:T(512)S(1)} %broadcast_multiply_fusion.2, f32[2048]{0:T(1024)S(1)} %bitcast.66, f32[2048]{0:T(1024)S(1)} %broadcast_subtract_fusion, f32[2048]{0:T(1024)S(1)} %bitcast.70, ...), kind=kOutput, calls=%fused_computation.12 | convolution fusion | flops 135327744 | bytes 4532228 | tf_op jit(solution)/shard_map/dot_general | solution.py:116
  (38 shorter events, 3.0 us)
Async XLA Ops:
  3.4 6.5 %collective-permute-start.1 = (bf16[16,1,2048]{2,0,1:T(8,128)(2,1)S(1)}, bf16[16,1,2048]{2,0,1:T(8,128)(2,1)S(1)}, u32[]{:S(2)}, u32[]{:S(2)}) collective-permute-start(bf16[16,1,2048]{2,0,1:T(8,128)(2,1)S(1)} %get-tuple-element.11), channel_id=1, source_target_pairs={{1,0},{2,1},{3,2},{4,3},{5,4},{6,5},{7,6},{9,8},{10,9},{11,10},{12... | collective-permute-start | bytes 196616 | tf_op jit(solution)/shard_map/ppermute | solution.py:25
  4.7 6.3 %collective-permute-start = (bf16[16,1,2048]{2,0,1:T(8,128)(2,1)S(1)}, bf16[16,1,2048]{2,0,1:T(8,128)(2,1)S(1)}, u32[]{:S(2)}, u32[]{:S(2)}) collective-permute-start(bf16[16,1,2048]{2,0,1:T(8,128)(2,1)S(1)} %get-tuple-element.10), channel_id=1, source_target_pairs={{0,1},{1,2},{2,3},{3,4},{4,5},{5,6},{6,7},{8,9},{9,10},{10,11},{11... | collective-permute-start | bytes 196616 | tf_op jit(solution)/shard_map/ppermute | solution.py:22
  11.4 2.0 %copy-start = (f32[16,34,2048]{2,0,1:T(8,128)}, f32[16,34,2048]{2,0,1:T(8,128)S(1)}, u32[]{:S(2)}) copy-start(f32[16,34,2048]{2,0,1:T(8,128)S(1)} %maximum_convert_fusion) | copy-start | bytes 13369348
  78.4 9.0 %copy-start.6 = (u32[256]{0:T(256)S(1)}, u32[256]{0:T(256)}, u32[]{:S(2)}) copy-start(u32[256]{0:T(256)} %constant.298) | copy-start | bytes 3076
  78.4 11.1 %copy-start.3 = (f32[1,1,2048]{2,1,0:T(1,128)S(1)}, f32[1,1,2048]{2,1,0:T(1,128)}, u32[]{:S(2)}) copy-start(f32[1,1,2048]{2,1,0:T(1,128)} %param.7) | copy-start | bytes 24580
  78.4 11.2 %copy-start.2 = (s32[1,1,2048]{2,1,0:T(1,128)S(1)}, s32[1,1,2048]{2,1,0:T(1,128)}, u32[]{:S(2)}) copy-start(s32[1,1,2048]{2,1,0:T(1,128)} %param.11) | copy-start | bytes 24580
  78.4 11.3 %copy-start.4 = (s32[1,1,2048]{2,1,0:T(1,128)S(1)}, s32[1,1,2048]{2,1,0:T(1,128)}, u32[]{:S(2)}) copy-start(s32[1,1,2048]{2,1,0:T(1,128)} %param.10) | copy-start | bytes 24580
  78.4 11.3 %copy-start.5 = (f32[1,1,2048]{2,1,0:T(1,128)S(1)}, f32[1,1,2048]{2,1,0:T(1,128)}, u32[]{:S(2)}) copy-start(f32[1,1,2048]{2,1,0:T(1,128)} %param.8) | copy-start | bytes 24580
  78.4 37.7 %copy-start.1 = (f32[10,1,1,2048]{3,2,1,0:T(1,128)S(1)}, f32[10,1,1,2048]{3,2,1,0:T(1,128)}, u32[]{:S(2)}) copy-start(f32[10,1,1,2048]{3,2,1,0:T(1,128)} %param.9) | copy-start | bytes 245764
  78.4 36.7 %all-to-all-start = ((bf16[16,32,2048]{2,0,1:T(8,128)(2,1)}), bf16[16,32,2048]{2,0,1:T(8,128)(2,1)S(1)}, u32[]{:S(2)}, u32[]{:S(2)}) async-start(bf16[16,32,2048]{2,0,1:T(8,128)(2,1)} %fusion.4), calls=%async_computation | async-start | bytes 4194304 | tf_op jit(solution)/shard_map/all_to_all | solution.py:96
where the time goes:
time: 205 us; the launch traced here: 203 us
  blocking collectives  64.4 us (31%)
  other arithmetic  48.4 us (24%)
  local copies, waits for them, and re-layouts  39.4 us (19%)
  waiting for transfers between devices  26.6 us (13%)
  starting transfers between devices  15.1 us (7%)
  matrix products  7.11 us (3%)
    unnamed x1, blocking collectives  64.4 us
    all_to_all x1, waiting for transfers between devices, body(): lax.all_to_all(advect_block(extended, own_x, own_y, own_z), 'vel', split_...  25.4 us
    scatter-add x1, other arithmetic, body(): jax.ops.segment_sum(sensitivity, group_slot, num_segments=PATCH_DEV * vel...  14.7 us
    convert_element_type x1, other arithmetic, advect_block(): return mixed.astype(jnp.bfloat16)  12.6 us
    concatenate x1, other arithmetic, advect_block(): jnp.roll(grid_form, -1, 3)  10.6 us
    all_to_all x1, starting transfers between devices, body(): lax.all_to_all(advect_block(extended, own_x, own_y, own_z), 'vel', split_...  8.85 us
    concatenate x1, other arithmetic, advect_block(): jnp.roll(grid_form, -1, 2)  8.34 us
    slice x2, local copies, waits for them, and re-layouts, advect_block(): jnp.roll(grid_form, 1, 3)  8.34 us
  transfers between devices with their start and end apart: 3, of which 2 were waited for; matrix products, arithmetic and copies ran while one was open for 1% of the time, Pallas kernels for 0%

commit v1 on v0

v1 whole, which is shorter than its diff:
```python
import jax
import jax.numpy as jnp
from jax import lax
from jax.experimental import pallas as pl
from jax.experimental.pallas import tpu as pltpu
from jax.sharding import PartitionSpec as P

NV = 8
MOMENTS = 10
PY = 16
PZ = 128
PATCH_DEV = 16
Q = 512
XB = 32
CELLS = PY * PZ
COURANT = 0.3

VEL = 32
GRP = 8
LOCAL = Q // VEL
CHUNKS = 4
WIDTH = CELLS // CHUNKS
ROWS = 128
STEP = 13

MESH = pl.DeviceIdType.MESH
F32 = jnp.float32
BF16 = jnp.bfloat16


def component(digit):
    sign = jnp.where((digit & 1) == 0, -1.0, 1.0).astype(F32)
    return sign * ((digit >> 1).astype(F32) + 0.5) / (NV / 2.0 - 0.5)


def velocities(vel_index):
    return (
        component(vel_index & (NV - 1)),
        component((vel_index >> 3) & (NV - 1)),
        component(vel_index >> 6),
    )


def poly(k, ux, uy, uz):
    third = 1.0 / 3.0
    terms = (
        jnp.ones_like(ux),
        ux,
        uy,
        uz,
        ux * ux - third,
        uy * uy - third,
        uz * uz - third,
        ux * uy,
        ux * uz,
        uy * uz,
    )
    value = jnp.zeros_like(ux)
    for i, term in enumerate(terms):
        value = jnp.where(k == i, term, value)
    return value


def split(value):
    high = value.astype(BF16)
    return high, (value - high.astype(F32)).astype(BF16)


def kernel(
    adj_hbm, relax_hbm, react_hbm, base_hbm, kind_hbm, patch_hbm,
    out_hbm, grad_out,
    xin, turned, staged, mu, result, relax, react, base, kind, patch,
    absorb_tab, etab, btab, part, part_in, total,
    load_sem, small_sem, halo_send, halo_recv, send_sem, recv_sem, out_sem, psend_sem, precv_sem,
):
    v = lax.axis_index("vel")
    g = lax.axis_index("grp")
    core = v & 1

    load = pltpu.make_async_copy(adj_hbm.at[:, 0], xin, load_sem)
    load.start()
    smalls = [
        pltpu.make_async_copy(relax_hbm.at[0], relax, small_sem.at[0]),
        pltpu.make_async_copy(react_hbm.at[0], react, small_sem.at[1]),
        pltpu.make_async_copy(kind_hbm.at[0], kind, small_sem.at[2]),
        pltpu.make_async_copy(patch_hbm.at[0], patch, small_sem.at[3]),
        pltpu.make_async_copy(base_hbm.at[:, 0], base, small_sem.at[4]),
    ]
    for copy in smalls:
        copy.start()

    barrier = pltpu.get_barrier_semaphore()

    def greet(k, _):
        pl.semaphore_signal(barrier, inc=1, device_id={"vel": (v + k) & (VEL - 1)}, device_id_type=MESH)
        return 0

    lax.fori_loop(1, VEL, greet, 0)

    @pl.when(g > 0)
    def _():
        pl.semaphore_signal(barrier, inc=1, device_id={"grp": g - 1}, device_id_type=MESH)

    @pl.when(g < GRP - 1)
    def _():
        pl.semaphore_signal(barrier, inc=1, device_id={"grp": g + 1}, device_id_type=MESH)

    row = lax.broadcasted_iota(jnp.int32, (256, 256), 0)
    col = lax.broadcasted_iota(jnp.int32, (256, 256), 1)
    perm = jnp.where(col == ((row & 15) << 4) + (row >> 4), 1.0, 0.0).astype(BF16)
    load.wait()
    for t in range(2):
        for c in range(CHUNKS):
            cols = pl.ds(c * WIDTH, WIDTH)
            block = xin[:, pl.ds(16 * t, 16), cols].reshape(256, WIDTH)
            moved = jnp.dot(perm, block, preferred_element_type=F32).astype(BF16)
            turned[pl.ds(1 + 16 * t, 16), :, cols] = moved.reshape(16, LOCAL, WIDTH)

    neighbours = jnp.where(g > 0, 1, 0) + jnp.where(g < GRP - 1, 1, 0)
    pl.semaphore_wait(barrier, VEL - 1 + neighbours)

    def to_lower():
        return pltpu.make_async_remote_copy(
            src_ref=turned.at[1], dst_ref=turned.at[XB + 1], send_sem=halo_send.at[0], recv_sem=halo_recv.at[0],
            device_id={"grp": g - 1}, device_id_type=MESH,
        )

    def to_upper():
        return pltpu.make_async_remote_copy(
            src_ref=turned.at[XB], dst_ref=turned.at[0], send_sem=halo_send.at[1], recv_sem=halo_recv.at[1],
            device_id={"grp": g + 1}, device_id_type=MESH,
        )

    @pl.when(g > 0)
    def _():
        to_lower().start()

    @pl.when(g < GRP - 1)
    def _():
        to_upper().start()

    @pl.when(g == 0)
    def _():
        turned[0] = jnp.zeros((LOCAL, CELLS), BF16)

    @pl.when(g == GRP - 1)
    def _():
        turned[XB + 1] = jnp.zeros((LOCAL, CELLS), BF16)

    own = v * LOCAL + lax.broadcasted_iota(jnp.int32, (LOCAL, PZ), 0)
    ux, uy, uz = velocities(own)
    rate_x, rate_y, rate_z = COURANT * jnp.abs(ux), COURANT * jnp.abs(uy), COURANT * jnp.abs(uz)
    rest = 1.0 - rate_x - rate_y - rate_z
    forward_x = ux > 0
    half = LOCAL // 2
    shift_z = jnp.where(((v >> 2) & 1) == 1, PZ - 1, 1)

    def advect(layer, c, store):
        count = WIDTH // PZ

        def cells(at, j):
            return turned[at, :, pl.ds((j % PY) * PZ, PZ)].astype(F32)

        centre = [cells(layer + 1, c * count + j) for j in range(-1, count + 1)]
        for j in range(count):
            block = centre[j + 1]
            along_x = jnp.where(forward_x, cells(layer + 2, c * count + j), cells(layer, c * count + j))
            along_y = jnp.concatenate([centre[j][:half], centre[j + 2][half:]], axis=0)
            along_z = pltpu.roll(block, shift_z, 1)
            value = rest * block + rate_x * along_x + rate_y * along_y + rate_z * along_z
            store(pl.ds((c * count + j) * PZ, PZ), value.astype(BF16))

    def target(k):
        o = (k * STEP) & (VEL - 1)
        da, db, dc = (o >> 1) & 3, o >> 3, o & 1
        dx = jnp.where(core == 0, da, db)
        dy = jnp.where(core == 0, db, da)
        y, x = v >> 3, (v >> 1) & 3
        return (((y + dy) & 3) << 3) + (((x + dx) & 3) << 1) + ((core + dc) & 1)

    own_rows = pl.ds(pl.multiple_of(v * LOCAL, LOCAL), LOCAL)

    def advect_and_send(layer, c):
        cols = pl.ds(c * WIDTH, WIDTH)

        def store(at, value):
            staged[layer, :, at] = value

        advect(layer, c, store)
        pltpu.make_async_remote_copy(
            src_ref=staged.at[layer, :, cols], dst_ref=mu.at[own_rows, cols], send_sem=send_sem, recv_sem=recv_sem.at[c],
            device_id={"vel": layer}, device_id_type=MESH,
        ).start()

    for c in range(CHUNKS):

        def step(k, _):
            layer = target(k)
            if c == 0:

                @pl.when((layer > 0) & (layer < XB - 1))
                def _():
                    advect_and_send(layer, c)
            else:
                advect_and_send(layer, c)
            return 0

        lax.fori_loop(1, VEL, step, 0)
        if c == 0:

            @pl.when(g > 0)
            def _():
                to_upper().wait_recv()

            @pl.when(g < GRP - 1)
            def _():
                to_lower().wait_recv()

            for layer in (0, XB - 1):

                @pl.when(v != layer)
                def _():
                    advect_and_send(layer, 0)

    def store_own(at, value):
        mu[own_rows, at] = value

    for c in range(CHUNKS):
        advect(v, c, store_own)

    q_row = lax.broadcasted_iota(jnp.int32, (64, Q), 1)
    j_row = lax.broadcasted_iota(jnp.int32, (64, Q), 0)
    ux, uy, uz = velocities(q_row)
    speed = ux * ux + uy * uy + uz * uz
    weight = jnp.exp(-speed)
    total_weight = jnp.sum(weight[0:8], axis=1, keepdims=True)[0:1]
    entry = poly(j_row & 15, ux, uy, uz) * jnp.where((j_row & 16) == 0, weight, weight * (speed / 3.0))
    high = entry.astype(BF16).astype(F32)
    etab[...] = jnp.where(j_row < 32, high, entry - high).astype(BF16)

    for r in range(Q // ROWS):
        rows = pl.ds(r * ROWS, ROWS)
        q_col = r * ROWS + lax.broadcasted_iota(jnp.int32, (ROWS, 128), 0)
        j_col = lax.broadcasted_iota(jnp.int32, (ROWS, 128), 1)
        ux, uy, uz = velocities(q_col)
        absorb_tab[rows, :] = (ux * ux + uy * uy + uz * uz) / 3.0
        entry = poly(j_col & 15, ux, uy, uz)
        high = entry.astype(BF16).astype(F32)
        btab[rows, :] = jnp.where((j_col & 16) == 0, high, entry - high).astype(BF16)

    for copy in smalls:
        copy.wait()

    total[...] = jnp.zeros((VEL, 128), F32)
    for c in range(CHUNKS):
        cols = pl.ds(c * WIDTH, WIDTH)
        arrived = mu.at[pl.ds(0, (VEL - 1) * LOCAL), cols]
        pltpu.make_async_copy(arrived, arrived, recv_sem.at[c]).wait()
        product = jnp.dot(etab[...], mu[:, cols], preferred_element_type=F32)
        first = product[0:16] + product[32:48]
        second = product[16:32] + product[48:64]
        kind_c = kind[:, cols]
        wall = jnp.where(kind_c == 2, react[:, cols], 0.0)
        fluid = jnp.where(kind_c != 0, 1.0, 0.0)
        relax_c = relax[:, cols]

        acc = base[0, :, cols] * second[0:1]
        for k in range(1, MOMENTS):
            acc = acc + base[k, :, cols] * second[k : k + 1]
        sens = -wall * acc / total_weight
        patch_c = patch[:, cols]
        owner = lax.broadcasted_iota(jnp.int32, (VEL, WIDTH), 0) == (patch_c >> 7)
        spread = jnp.where(owner, sens, 0.0)
        piece0 = spread.astype(BF16)
        left = spread - piece0.astype(F32)
        piece1 = left.astype(BF16)
        piece2 = (left - piece1.astype(F32)).astype(BF16)
        slot = lax.broadcasted_iota(jnp.int32, (128, WIDTH), 0) == (patch_c & 15)
        sums = lax.dot_general(
            jnp.concatenate([piece0, piece1, piece2], axis=0),
            jnp.where(slot, 1.0, 0.0).astype(BF16),
            (((1,), (1,)), ((), ())),
            preferred_element_type=F32,
        )
        total[...] += sums[0:VEL] + sums[VEL : 2 * VEL] + sums[2 * VEL :]
        if c == CHUNKS - 1:
            for i in range(VEL):
                part[i] = total[i : i + 1]

            def give(k, _):
                owner = target(k)
                pltpu.make_async_remote_copy(
                    src_ref=part.at[owner], dst_ref=part_in.at[v], send_sem=psend_sem, recv_sem=precv_sem,
                    device_id={"vel": owner}, device_id_type=MESH,
                ).start()
                return 0

            lax.fori_loop(1, VEL, give, 0)

        moments = (fluid * relax_c) * ((first - wall * second) / total_weight)
        high, low = split(moments)
        stacked = jnp.concatenate([high, high, low, low], axis=0)
        keep = fluid * (1.0 - relax_c)
        keep_wall = keep * wall
        for r in range(Q // ROWS):
            rows = pl.ds(r * ROWS, ROWS)
            collided = jnp.dot(btab[rows, 0:64], stacked, preferred_element_type=F32)
            for j in range(WIDTH // 128):
                sub = slice(j * 128, (j + 1) * 128)
                at = pl.ds(c * WIDTH + j * 128, 128)
                factor = keep[:, sub] - keep_wall[:, sub] * absorb_tab[rows, :]
                value = factor * mu[rows, at].astype(F32) + collided[:, sub]
                result[rows, at] = value.astype(BF16)
        pltpu.make_async_copy(result.at[:, cols], out_hbm.at[:, cols], out_sem.at[c]).start()

    part_in[pl.ds(v, 1)] = part[pl.ds(v, 1)]
    sent = part.at[pl.ds(0, VEL - 1)]
    pltpu.make_async_copy(sent, sent, precv_sem).wait()
    grad = part_in[0]
    for i in range(1, VEL):
        grad = grad + part_in[i]
    grad_out[...] = grad

    pltpu.make_async_copy(sent, sent, psend_sem).wait()
    staged_out = staged.at[pl.ds(0, VEL - 1)]
    pltpu.make_async_copy(staged_out, staged_out, send_sem).wait()

    @pl.when(g > 0)
    def _():
        to_lower().wait_send()

    @pl.when(g < GRP - 1)
    def _():
        to_upper().wait_send()

    for c in range(CHUNKS):
        cols = pl.ds(c * WIDTH, WIDTH)
        pltpu.make_async_copy(result.at[:, cols], out_hbm.at[:, cols], out_sem.at[c]).wait()


def body(adjoint, relaxation, reaction, base_moments, cell_kind, patch_id):
    anywhere = pl.BlockSpec(memory_space=pl.ANY)
    dma = pltpu.SemaphoreType.DMA
    out, grad = pl.pallas_call(
        kernel,
        out_shape=(jax.ShapeDtypeStruct((Q, CELLS), BF16), jax.ShapeDtypeStruct((1, 128), F32)),
        in_specs=[anywhere] * 6,
        out_specs=(anywhere, pl.BlockSpec(memory_space=pltpu.VMEM)),
        scratch_shapes=[
            pltpu.VMEM((LOCAL, XB, CELLS), BF16),
            pltpu.VMEM((XB + 2, LOCAL, CELLS), BF16),
            pltpu.VMEM((XB, LOCAL, CELLS), BF16),
            pltpu.VMEM((Q, CELLS), BF16),
            pltpu.VMEM((Q, CELLS), BF16),
            pltpu.VMEM((1, CELLS), F32),
            pltpu.VMEM((1, CELLS), F32),
            pltpu.VMEM((MOMENTS, 1, CELLS), F32),
            pltpu.VMEM((1, CELLS), jnp.int32),
            pltpu.VMEM((1, CELLS), jnp.int32),
            pltpu.VMEM((Q, 128), F32),
            pltpu.VMEM((64, Q), BF16),
            pltpu.VMEM((Q, 128), BF16),
            pltpu.VMEM((VEL, 1, 128), F32),
            pltpu.VMEM((VEL, 1, 128), F32),
            pltpu.VMEM((VEL, 128), F32),
            dma,
            dma((5,)),
            dma((2,)),
            dma((2,)),
            dma,
            dma((CHUNKS,)),
            dma((CHUNKS,)),
            dma,
            dma,
        ],
        compiler_params=pltpu.CompilerParams(
            collective_id=0, has_side_effects=True, vmem_limit_bytes=60 * 1024 * 1024
        ),
        name="adjoint_step",
    )(adjoint, relaxation, reaction, base_moments, cell_kind, patch_id)
    return out.reshape(Q, 1, 1, CELLS), grad[0, :PATCH_DEV]


def solution(mesh):
    placed = (
        P("vel", "grp", None, None),
        P("grp", "vel", None),
        P("grp", "vel", None),
        P(None, "grp", "vel", None),
        P("grp", "vel", None),
        P("grp", "vel", None),
    )
    return jax.shard_map(
        body,
        mesh=mesh,
        in_specs=placed,
        out_specs=(P(None, "grp", "vel", None), P(("vel", "grp"))),
        check_vma=False,
    )
```

time: 205 us -> 44.2 us (0.22); the launches traced: 203 us -> 44 us
  blocking collectives: 64.4 us -> 0 us
  other arithmetic: 48.4 us -> 0 us
  Pallas kernels: 0 us -> 39.1 us
  local copies, waits for them, and re-layouts: 39.4 us -> 4.3 us
  waiting for transfers between devices: 26.6 us -> 0 us
  starting transfers between devices: 15.1 us -> 0 us
  matrix products: 7.11 us -> 0 us
    unnamed x1 -> x0, blocking collectives: 64.4 us -> none
    pallas_call x0 -> x1, Pallas kernels: none -> 39.1 us  [body(): pl.pallas_call(kernel, out_shape=(jax.ShapeDtypeStruct((Q, CELLS), BF16),...]
    all_to_all x1 -> x0, waiting for transfers between devices: 25.4 us -> none  [body(): lax.all_to_all(advect_block(extended, own_x, own_y, own_z), 'vel', split_...]
    concatenate x4 -> x0, local copies, waits for them, and re-layouts: 19.7 us -> none  [the longest x1 4.97 us: advect_block(): jnp.roll(grid_form, -1, 3)]
    concatenate x2 -> x0, other arithmetic: 18.9 us -> none  [the longest x1 10.6 us: advect_block(): jnp.roll(grid_form, -1, 3)]
    scatter-add x1 -> x0, other arithmetic: 14.7 us -> none  [body(): jax.ops.segment_sum(sensitivity, group_slot, num_segments=PATCH_DEV * vel...]
    slice x6 -> x0, local copies, waits for them, and re-layouts: 13.3 us -> none  [the longest x2 8.34 us: advect_block(): jnp.roll(grid_form, 1, 3)]
    convert_element_type x2 -> x0, other arithmetic: 13 us -> none  [the longest x1 12.6 us: advect_block(): return mixed.astype(jnp.bfloat16)]
  transfers between devices with their start and end apart: 3 -> 0, of which waited for: 2 -> 0; matrix products, arithmetic and copies ran while one was open for 1% -> 0% of each run, Pallas kernels for 0% -> 0%
where the time goes in v1:
time: 44.2 us; the launch traced here: 44 us
  Pallas kernels  39.1 us (88%)
  local copies, waits for them, and re-layouts  4.3 us (10%)
  between operations  0.64 us (1%)
    pallas_call x1, Pallas kernels, body(): pl.pallas_call(kernel, out_shape=(jax.ShapeDtypeStruct((Q, CELLS), BF16),...  39.1 us
    unnamed x1, local copies, waits for them, and re-layouts  3.16 us
    squeeze x1, local copies, waits for them, and re-layouts, body(): return (out.reshape(Q, 1, 1, CELLS), grad[0, :PATCH_DEV])  1.14 us

profile of v1, /device:TPU:1, one launch (start us, length us, event | category | flops | bytes accessed | tf_op | source)
XLA Modules:
  0.0 44.0 jit_solution(18173180641016280645)
XLA Ops:
  0.6 39.1 %adjoint_step.1 = (bf16[512,2048]{1,0:T(8,128)(2,1)}, f32[1,128]{1,0:T(1,128)}) custom-call(bf16[16,1,32,2048]{3,2,1,0:T(8,128)(2,1)} %adj_hbm.1, f32[1,1,2048]{2,1,0:T(1,128)} %relax_hbm.1, f32[1,1,2048]{2,1,0:T(1,128)} %react_hbm.1, f32[10,1,1,2048]{3,2,1,0:T(1,128)} %base_hbm.1, s32[1,1,2048]{2,1,0:T(1,128)} %kind_hbm.1, s32[1,1,2048]{2,1,0:T(1,128)} %patch_hbm.1), custom_call_target="tpu_custom_call" | custom-call | tf_op jit(solution)/shard_map/adjoint_step/pallas_call | solution.py:344
  39.7 1.1 %slice_bitcast_fusion = f32[16]{0:T(128)} fusion(f32[1,128]{1,0:T(1,128)} %get-tuple-element.5), kind=kLoop, calls=%fused_computation | loop fusion | bytes 128 | tf_op jit(solution)/shard_map/squeeze | solution.py:381
  40.9 3.2 %copy.9 = bf16[512,1,1,2048]{3,0,2,1:T(8,128)(2,1)} copy(bf16[512,1,1,2048]{3,0,2,1:T(8,128)(2,1)} %bitcast.3) | data formatting | bytes 4194304

commit v2 on v1

--- a/solution.py
+++ b/solution.py
@@ -68,10 +68,10 @@
 
 def kernel(
     adj_hbm, relax_hbm, react_hbm, base_hbm, kind_hbm, patch_hbm,
-    out_hbm, grad_out,
-    xin, turned, staged, mu, result, relax, react, base, kind, patch,
+    result, grad_out,
+    xin, turned, staged, mu, relax, react, base, kind, patch,
     absorb_tab, etab, btab, part, part_in, total,
-    load_sem, small_sem, halo_send, halo_recv, send_sem, recv_sem, out_sem, psend_sem, precv_sem,
+    load_sem, small_sem, halo_send, halo_recv, send_sem, recv_sem, psend_sem, precv_sem,
 ):
     v = lax.axis_index("vel")
     g = lax.axis_index("grp")
@@ -311,7 +311,6 @@
                 factor = keep[:, sub] - keep_wall[:, sub] * absorb_tab[rows, :]
                 value = factor * mu[rows, at].astype(F32) + collided[:, sub]
                 result[rows, at] = value.astype(BF16)
-        pltpu.make_async_copy(result.at[:, cols], out_hbm.at[:, cols], out_sem.at[c]).start()
 
     part_in[pl.ds(v, 1)] = part[pl.ds(v, 1)]
     sent = part.at[pl.ds(0, VEL - 1)]
@@ -333,24 +332,43 @@
     def _():
         to_upper().wait_send()
 
+
+def store_kernel(result, grad, out_hbm, grad_hbm, small, out_sem, grad_sem):
+    copies = []
     for c in range(CHUNKS):
-        cols = pl.ds(c * WIDTH, WIDTH)
-        pltpu.make_async_copy(result.at[:, cols], out_hbm.at[:, cols], out_sem.at[c]).wait()
+        rows = pl.ds(c * (Q // CHUNKS), Q // CHUNKS)
+        copies.append(pltpu.make_async_copy(result.at[rows], out_hbm.at[rows], out_sem.at[c]))
+    for copy in copies:
+        copy.start()
+    small[...] = grad[:, 0:PATCH_DEV]
+    last = pltpu.make_async_copy(small, grad_hbm, grad_sem)
+    last.start()
+    for copy in copies:
+        copy.wait()
+    last.wait()
+
+
+def in_hbm(x):
+    return pltpu.with_memory_space_constraint(x, pltpu.HBM)
+
+
+def in_vmem(x):
+    return pltpu.with_memory_space_constraint(x, pltpu.VMEM)
 
 
 def body(adjoint, relaxation, reaction, base_moments, cell_kind, patch_id):
-    anywhere = pl.BlockSpec(memory_space=pl.ANY)
     dma = pltpu.SemaphoreType.DMA
-    out, grad = pl.pallas_call(
+    hbm = pl.BlockSpec(memory_space=pltpu.HBM)
+    vmem = pl.BlockSpec(memory_space=pltpu.VMEM)
+    result, grad = pl.pallas_call(
         kernel,
-        out_shape=(jax.ShapeDtypeStruct((Q, CELLS), BF16), jax.ShapeDtypeStruct((1, 128), F32)),
-        in_specs=[anywhere] * 6,
-        out_specs=(anywhere, pl.BlockSpec(memory_space=pltpu.VMEM)),
+        out_shape=(pltpu.VMEM((Q, CELLS), BF16), pltpu.VMEM((1, 128), F32)),
+        in_specs=[hbm] * 6,
+        out_specs=(vmem, vmem),
         scratch_shapes=[
             pltpu.VMEM((LOCAL, XB, CELLS), BF16),
             pltpu.VMEM((XB + 2, LOCAL, CELLS), BF16),
             pltpu.VMEM((XB, LOCAL, CELLS), BF16),
-            pltpu.VMEM((Q, CELLS), BF16),
             pltpu.VMEM((Q, CELLS), BF16),
             pltpu.VMEM((1, CELLS), F32),
             pltpu.VMEM((1, CELLS), F32),
@@ -369,16 +387,24 @@
             dma((2,)),
             dma,
             dma((CHUNKS,)),
-            dma((CHUNKS,)),
             dma,
             dma,
         ],
         compiler_params=pltpu.CompilerParams(
-            collective_id=0, has_side_effects=True, vmem_limit_bytes=60 * 1024 * 1024
+            collective_id=0, has_side_effects=True, vmem_limit_bytes=40 * 1024 * 1024
         ),
         name="adjoint_step",
-    )(adjoint, relaxation, reaction, base_moments, cell_kind, patch_id)
-    return out.reshape(Q, 1, 1, CELLS), grad[0, :PATCH_DEV]
+    )(*[in_hbm(x) for x in (adjoint, relaxation, reaction, base_moments, cell_kind, patch_id)])
+    out, grad = pl.pallas_call(
+        store_kernel,
+        out_shape=(jax.ShapeDtypeStruct((Q, CELLS), BF16), jax.ShapeDtypeStruct((1, PATCH_DEV), F32)),
+        in_specs=[vmem] * 2,
+        out_specs=(hbm, hbm),
+        scratch_shapes=[pltpu.VMEM((1, PATCH_DEV), F32), dma((CHUNKS,)), dma],
+        compiler_params=pltpu.CompilerParams(vmem_limit_bytes=8 * 1024 * 1024),
+        name="store_step",
+    )(in_vmem(result), in_vmem(grad))
+    return out.reshape(Q, 1, 1, CELLS), grad.reshape(PATCH_DEV)
 
 
 def solution(mesh):

time: 44.2 us -> 40.6 us (0.919)
  local copies, waits for them, and re-layouts: 4.3 us -> 0 us
  Pallas kernels: 39.1 us -> 39.9 us
    unnamed x1 -> x0, local copies, waits for them, and re-layouts: 3.16 us -> none
    squeeze x1 -> x0, local copies, waits for them, and re-layouts: 1.14 us -> none  [body(): return (out.reshape(Q, 1, 1, CELLS), grad[0, :PATCH_DEV])]
    pallas_call x1 -> x2, Pallas kernels: 39.1 us -> 39.9 us  [the longest x1 38.5 us: body(): pl.pallas_call(kernel, out_shape=(pltpu.VMEM((Q, CELLS), BF16), pltpu.VME...]
where the time goes in v2:
time: 40.6 us; the launch traced here: 40.5 us
  Pallas kernels  39.9 us (98%)
  between operations  0.64 us (2%)
    pallas_call x1, Pallas kernels, body(): pl.pallas_call(kernel, out_shape=(pltpu.VMEM((Q, CELLS), BF16), pltpu.VME...  38.5 us
    pallas_call x1, Pallas kernels, body(): pl.pallas_call(store_kernel, out_shape=(jax.ShapeDtypeStruct((Q, CELLS),...  1.36 us

profile of v2, /device:TPU:1, one launch (start us, length us, event | category | flops | bytes accessed | tf_op | source)
XLA Modules:
  0.0 40.5 jit_solution(11508516255642828967)
XLA Ops:
  0.6 38.5 %adjoint_step.1 = (bf16[512,2048]{1,0:T(8,128)(2,1)S(1)}, f32[1,128]{1,0:T(1,128)S(1)}) custom-call(bf16[16,1,32,2048]{3,2,1,0:T(8,128)(2,1)} %adj_hbm.1, f32[1,1,2048]{2,1,0:T(1,128)} %relax_hbm.1, f32[1,1,2048]{2,1,0:T(1,128)} %react_hbm.1, f32[10,1,1,2048]{3,2,1,0:T(1,128)} %base_hbm.1, s32[1,1,2048]{2,1,0:T(1,128)} %kind_hbm.1, s32[1,1,2048]{2,1,0:T(1,128)} %patch_hbm.1), custom_call_target="tpu_custom_call" | custom-call | tf_op jit(solution)/shard_map/adjoint_step/pallas_call | solution.py:363
  39.1 1.4 %store_step.1 = (bf16[512,2048]{1,0:T(8,128)(2,1)}, f32[1,16]{1,0:T(1,128)}) custom-call(bf16[512,2048]{1,0:T(8,128)(2,1)S(1)} %get-tuple-element.6.result, f32[1,128]{1,0:T(1,128)S(1)} %get-tuple-element.7.grad), custom_call_target="tpu_custom_call" | custom-call | tf_op jit(solution)/shard_map/store_step/pallas_call | solution.py:398

commit v3 on v2

--- a/solution.py
+++ b/solution.py
@@ -18,9 +18,14 @@
 VEL = 32
 GRP = 8
 LOCAL = Q // VEL
-CHUNKS = 4
-WIDTH = CELLS // CHUNKS
+WIDTHS = (512, 512, 512, 256, 256)
+STARTS = tuple(sum(WIDTHS[:i]) for i in range(len(WIDTHS)))
+CHUNKS = len(WIDTHS)
+EARLY = 2
+PIECES = ((0, 640), (1920, 128), (640, 640), (1280, 640))
+FIRST = 2
 ROWS = 128
+STORES = 4
 STEP = 13
 
 MESH = pl.DeviceIdType.MESH
@@ -77,8 +82,12 @@
     g = lax.axis_index("grp")
     core = v & 1
 
-    load = pltpu.make_async_copy(adj_hbm.at[:, 0], xin, load_sem)
-    load.start()
+    loads = []
+    for i, (start, width) in enumerate(PIECES):
+        cols = pl.ds(start, width)
+        loads.append(pltpu.make_async_copy(adj_hbm.at[:, 0, :, cols], xin.at[:, :, cols], load_sem.at[i]))
+    for copy in loads:
+        copy.start()
     smalls = [
         pltpu.make_async_copy(relax_hbm.at[0], relax, small_sem.at[0]),
         pltpu.make_async_copy(react_hbm.at[0], react, small_sem.at[1]),
@@ -108,13 +117,18 @@
     row = lax.broadcasted_iota(jnp.int32, (256, 256), 0)
     col = lax.broadcasted_iota(jnp.int32, (256, 256), 1)
     perm = jnp.where(col == ((row & 15) << 4) + (row >> 4), 1.0, 0.0).astype(BF16)
-    load.wait()
-    for t in range(2):
-        for c in range(CHUNKS):
-            cols = pl.ds(c * WIDTH, WIDTH)
-            block = xin[:, pl.ds(16 * t, 16), cols].reshape(256, WIDTH)
+
+    def turn(i):
+        start, width = PIECES[i]
+        cols = pl.ds(start, width)
+        loads[i].wait()
+        for t in range(2):
+            block = xin[:, pl.ds(16 * t, 16), cols].reshape(256, width)
             moved = jnp.dot(perm, block, preferred_element_type=F32).astype(BF16)
-            turned[pl.ds(1 + 16 * t, 16), :, cols] = moved.reshape(16, LOCAL, WIDTH)
+            turned[pl.ds(1 + 16 * t, 16), :, cols] = moved.reshape(16, LOCAL, width)
+
+    for i in range(FIRST):
+        turn(i)
 
     neighbours = jnp.where(g > 0, 1, 0) + jnp.where(g < GRP - 1, 1, 0)
     pl.semaphore_wait(barrier, VEL - 1 + neighbours)
@@ -131,21 +145,22 @@
             device_id={"grp": g + 1}, device_id_type=MESH,
         )
 
-    @pl.when(g > 0)
-    def _():
-        to_lower().start()
-
-    @pl.when(g < GRP - 1)
-    def _():
-        to_upper().start()
-
-    @pl.when(g == 0)
-    def _():
-        turned[0] = jnp.zeros((LOCAL, CELLS), BF16)
-
-    @pl.when(g == GRP - 1)
-    def _():
-        turned[XB + 1] = jnp.zeros((LOCAL, CELLS), BF16)
+    def send_ends():
+        @pl.when(g > 0)
+        def _():
+            to_lower().start()
+
+        @pl.when(g < GRP - 1)
+        def _():
+            to_upper().start()
+
+        @pl.when(g == 0)
+        def _():
+            turned[0] = jnp.zeros((LOCAL, CELLS), BF16)
+
+        @pl.when(g == GRP - 1)
+        def _():
+            turned[XB + 1] = jnp.zeros((LOCAL, CELLS), BF16)
 
     own = v * LOCAL + lax.broadcasted_iota(jnp.int32, (LOCAL, PZ), 0)
     ux, uy, uz = velocities(own)
@@ -156,19 +171,20 @@
     shift_z = jnp.where(((v >> 2) & 1) == 1, PZ - 1, 1)
 
     def advect(layer, c, store):
-        count = WIDTH // PZ
+        count = WIDTHS[c] // PZ
+        base_block = STARTS[c] // PZ
 
         def cells(at, j):
             return turned[at, :, pl.ds((j % PY) * PZ, PZ)].astype(F32)
 
-        centre = [cells(layer + 1, c * count + j) for j in range(-1, count + 1)]
+        centre = [cells(layer + 1, base_block + j) for j in range(-1, count + 1)]
         for j in range(count):
             block = centre[j + 1]
-            along_x = jnp.where(forward_x, cells(layer + 2, c * count + j), cells(layer, c * count + j))
+            along_x = jnp.where(forward_x, cells(layer + 2, base_block + j), cells(layer, base_block + j))
             along_y = jnp.concatenate([centre[j][:half], centre[j + 2][half:]], axis=0)
             along_z = pltpu.roll(block, shift_z, 1)
             value = rest * block + rate_x * along_x + rate_y * along_y + rate_z * along_z
-            store(pl.ds((c * count + j) * PZ, PZ), value.astype(BF16))
+            store(pl.ds((base_block + j) * PZ, PZ), value.astype(BF16))
 
     def target(k):
         o = (k * STEP) & (VEL - 1)
@@ -181,7 +197,7 @@
     own_rows = pl.ds(pl.multiple_of(v * LOCAL, LOCAL), LOCAL)
 
     def advect_and_send(layer, c):
-        cols = pl.ds(c * WIDTH, WIDTH)
+        cols = pl.ds(STARTS[c], WIDTHS[c])
 
         def store(at, value):
             staged[layer, :, at] = value
@@ -196,7 +212,7 @@
 
         def step(k, _):
             layer = target(k)
-            if c == 0:
+            if c < EARLY:
 
                 @pl.when((layer > 0) & (layer < XB - 1))
                 def _():
@@ -207,6 +223,10 @@
 
         lax.fori_loop(1, VEL, step, 0)
         if c == 0:
+            for i in range(FIRST, len(PIECES)):
+                turn(i)
+            send_ends()
+        if c == EARLY - 1:
 
             @pl.when(g > 0)
             def _():
@@ -220,7 +240,8 @@
 
                 @pl.when(v != layer)
                 def _():
-                    advect_and_send(layer, 0)
+                    for early in range(EARLY):
+                        advect_and_send(layer, early)
 
     def store_own(at, value):
         mu[own_rows, at] = value
@@ -253,7 +274,7 @@
 
     total[...] = jnp.zeros((VEL, 128), F32)
     for c in range(CHUNKS):
-        cols = pl.ds(c * WIDTH, WIDTH)
+        cols = pl.ds(STARTS[c], WIDTHS[c])
         arrived = mu.at[pl.ds(0, (VEL - 1) * LOCAL), cols]
         pltpu.make_async_copy(arrived, arrived, recv_sem.at[c]).wait()
         product = jnp.dot(etab[...], mu[:, cols], preferred_element_type=F32)
@@ -269,13 +290,13 @@
             acc = acc + base[k, :, cols] * second[k : k + 1]
         sens = -wall * acc / total_weight
         patch_c = patch[:, cols]
-        owner = lax.broadcasted_iota(jnp.int32, (VEL, WIDTH), 0) == (patch_c >> 7)
+        owner = lax.broadcasted_iota(jnp.int32, (VEL, WIDTHS[c]), 0) == (patch_c >> 7)
         spread = jnp.where(owner, sens, 0.0)
         piece0 = spread.astype(BF16)
         left = spread - piece0.astype(F32)
         piece1 = left.astype(BF16)
         piece2 = (left - piece1.astype(F32)).astype(BF16)
-        slot = lax.broadcasted_iota(jnp.int32, (128, WIDTH), 0) == (patch_c & 15)
+        slot = lax.broadcasted_iota(jnp.int32, (128, WIDTHS[c]), 0) == (patch_c & 15)
         sums = lax.dot_general(
             jnp.concatenate([piece0, piece1, piece2], axis=0),
             jnp.where(slot, 1.0, 0.0).astype(BF16),
@@ -305,9 +326,9 @@
         for r in range(Q // ROWS):
             rows = pl.ds(r * ROWS, ROWS)
             collided = jnp.dot(btab[rows, 0:64], stacked, preferred_element_type=F32)
-            for j in range(WIDTH // 128):
+            for j in range(WIDTHS[c] // 128):
                 sub = slice(j * 128, (j + 1) * 128)
-                at = pl.ds(c * WIDTH + j * 128, 128)
+                at = pl.ds(STARTS[c] + j * 128, 128)
                 factor = keep[:, sub] - keep_wall[:, sub] * absorb_tab[rows, :]
                 value = factor * mu[rows, at].astype(F32) + collided[:, sub]
                 result[rows, at] = value.astype(BF16)
@@ -335,8 +356,8 @@
 
 def store_kernel(result, grad, out_hbm, grad_hbm, small, out_sem, grad_sem):
     copies = []
-    for c in range(CHUNKS):
-        rows = pl.ds(c * (Q // CHUNKS), Q // CHUNKS)
+    for c in range(STORES):
+        rows = pl.ds(c * (Q // STORES), Q // STORES)
         copies.append(pltpu.make_async_copy(result.at[rows], out_hbm.at[rows], out_sem.at[c]))
     for copy in copies:
         copy.start()
@@ -381,7 +402,7 @@
             pltpu.VMEM((VEL, 1, 128), F32),
             pltpu.VMEM((VEL, 1, 128), F32),
             pltpu.VMEM((VEL, 128), F32),
-            dma,
+            dma((len(PIECES),)),
             dma((5,)),
             dma((2,)),
             dma((2,)),
@@ -400,7 +421,7 @@
         out_shape=(jax.ShapeDtypeStruct((Q, CELLS), BF16), jax.ShapeDtypeStruct((1, PATCH_DEV), F32)),
         in_specs=[vmem] * 2,
         out_specs=(hbm, hbm),
-        scratch_shapes=[pltpu.VMEM((1, PATCH_DEV), F32), dma((CHUNKS,)), dma],
+        scratch_shapes=[pltpu.VMEM((1, PATCH_DEV), F32), dma((STORES,)), dma],
         compiler_params=pltpu.CompilerParams(vmem_limit_bytes=8 * 1024 * 1024),
         name="store_step",
     )(in_vmem(result), in_vmem(grad))

time: 40.6 us -> 41.8 us (1.030)
  Pallas kernels: 39.9 us -> 40.9 us
    pallas_call x1, Pallas kernels: 38.5 us -> 39.5 us  [body(): pl.pallas_call(kernel, out_shape=(pltpu.VMEM((Q, CELLS), BF16), pltpu.VME...]
where the time goes in v3:
time: 41.8 us; the launch traced here: 41.5 us
  Pallas kernels  40.9 us (98%)
  between operations  0.64 us (2%)
    pallas_call x1, Pallas kernels, body(): pl.pallas_call(kernel, out_shape=(pltpu.VMEM((Q, CELLS), BF16), pltpu.VME...  39.5 us
    pallas_call x1, Pallas kernels, body(): pl.pallas_call(store_kernel, out_shape=(jax.ShapeDtypeStruct((Q, CELLS),...  1.36 us

profile of v3, /device:TPU:1, one launch (start us, length us, event | category | flops | bytes accessed | tf_op | source)
XLA Modules:
  0.0 41.5 jit_solution(131589711022551074)
XLA Ops:
  0.6 39.5 %adjoint_step.1 = (bf16[512,2048]{1,0:T(8,128)(2,1)S(1)}, f32[1,128]{1,0:T(1,128)S(1)}) custom-call(bf16[16,1,32,2048]{3,2,1,0:T(8,128)(2,1)} %adj_hbm.1, f32[1,1,2048]{2,1,0:T(1,128)} %relax_hbm.1, f32[1,1,2048]{2,1,0:T(1,128)} %react_hbm.1, f32[10,1,1,2048]{3,2,1,0:T(1,128)} %base_hbm.1, s32[1,1,2048]{2,1,0:T(1,128)} %kind_hbm.1, s32[1,1,2048]{2,1,0:T(1,128)} %patch_hbm.1), custom_call_target="tpu_custom_call" | custom-call | tf_op jit(solution)/shard_map/adjoint_step/pallas_call | solution.py:384
  40.2 1.4 %store_step.1 = (bf16[512,2048]{1,0:T(8,128)(2,1)}, f32[1,16]{1,0:T(1,128)}) custom-call(bf16[512,2048]{1,0:T(8,128)(2,1)S(1)} %get-tuple-element.6.result, f32[1,128]{1,0:T(1,128)S(1)} %get-tuple-element.7.grad), custom_call_target="tpu_custom_call" | custom-call | tf_op jit(solution)/shard_map/store_step/pallas_call | solution.py:419

commit v4 on v3

--- a/solution.py
+++ b/solution.py
@@ -18,15 +18,15 @@
 VEL = 32
 GRP = 8
 LOCAL = Q // VEL
-WIDTHS = (512, 512, 512, 256, 256)
+WIDTHS = (512, 512, 512, 512)
 STARTS = tuple(sum(WIDTHS[:i]) for i in range(len(WIDTHS)))
 CHUNKS = len(WIDTHS)
-EARLY = 2
-PIECES = ((0, 640), (1920, 128), (640, 640), (1280, 640))
-FIRST = 2
+PIECES = ((0, 512), (512, 512), (1024, 512), (1536, 512))
+CHIPS = (1, 4, 3, 12, 5, 15, 2, 8, 13, 7, 6, 9, 14, 11, 10)
+ONE, TWO, THREE, FOUR = (0, 4), (4, 10), (10, 14), (14, 15)
+PACKED = tuple(sum(chip << (4 * i) for i, chip in enumerate(CHIPS[at : at + 7])) for at in (0, 7, 14))
 ROWS = 128
 STORES = 4
-STEP = 13
 
 MESH = pl.DeviceIdType.MESH
 F32 = jnp.float32
@@ -76,7 +76,7 @@
     result, grad_out,
     xin, turned, staged, mu, relax, react, base, kind, patch,
     absorb_tab, etab, btab, part, part_in, total,
-    load_sem, small_sem, halo_send, halo_recv, send_sem, recv_sem, psend_sem, precv_sem,
+    round_sem, load_sem, small_sem, halo_send, halo_recv, send_sem, recv_sem, psend_sem, precv_sem,
 ):
     v = lax.axis_index("vel")
     g = lax.axis_index("grp")
@@ -98,13 +98,15 @@
     for copy in smalls:
         copy.start()
 
+    def device(dx, dy, dc):
+        y, x = v >> 3, (v >> 1) & 3
+        return (((y + dy) & 3) << 3) + (((x + dx) & 3) << 1) + ((core + dc) & 1)
+
     barrier = pltpu.get_barrier_semaphore()
-
-    def greet(k, _):
-        pl.semaphore_signal(barrier, inc=1, device_id={"vel": (v + k) & (VEL - 1)}, device_id_type=MESH)
-        return 0
-
-    lax.fori_loop(1, VEL, greet, 0)
+    hops = ((1, 0), (0, 1), (3, 0), (0, 3))
+    nearest = [(0, 0, 1)] + [(dx, dy, dc) for dx, dy in hops for dc in (0, 1)]
+    for at in nearest:
+        pl.semaphore_signal(barrier, inc=1, device_id={"vel": device(*at)}, device_id_type=MESH)
 
     @pl.when(g > 0)
     def _():
@@ -113,6 +115,13 @@
     @pl.when(g < GRP - 1)
     def _():
         pl.semaphore_signal(barrier, inc=1, device_id={"grp": g + 1}, device_id_type=MESH)
+
+    def tell(i):
+        for dx, dy in hops:
+            pl.semaphore_signal(round_sem.at[i], inc=1, device_id={"vel": device(dx, dy, 0)}, device_id_type=MESH)
+
+    def hear(i):
+        pl.semaphore_wait(round_sem.at[i], len(hops))
 
     row = lax.broadcasted_iota(jnp.int32, (256, 256), 0)
     col = lax.broadcasted_iota(jnp.int32, (256, 256), 1)
@@ -127,11 +136,12 @@
             moved = jnp.dot(perm, block, preferred_element_type=F32).astype(BF16)
             turned[pl.ds(1 + 16 * t, 16), :, cols] = moved.reshape(16, LOCAL, width)
 
-    for i in range(FIRST):
+    for i in range(len(PIECES)):
         turn(i)
 
     neighbours = jnp.where(g > 0, 1, 0) + jnp.where(g < GRP - 1, 1, 0)
-    pl.semaphore_wait(barrier, VEL - 1 + neighbours)
+    pl.semaphore_wait(barrier, len(nearest) + neighbours)
+    tell(0)
 
     def to_lower():
         return pltpu.make_async_remote_copy(
@@ -145,22 +155,21 @@
             device_id={"grp": g + 1}, device_id_type=MESH,
         )
 
-    def send_ends():
-        @pl.when(g > 0)
-        def _():
-            to_lower().start()
-
-        @pl.when(g < GRP - 1)
-        def _():
-            to_upper().start()
-
-        @pl.when(g == 0)
-        def _():
-            turned[0] = jnp.zeros((LOCAL, CELLS), BF16)
-
-        @pl.when(g == GRP - 1)
-        def _():
-            turned[XB + 1] = jnp.zeros((LOCAL, CELLS), BF16)
+    @pl.when(g > 0)
+    def _():
+        to_lower().start()
+
+    @pl.when(g < GRP - 1)
+    def _():
+        to_upper().start()
+
+    @pl.when(g == 0)
+    def _():
+        turned[0] = jnp.zeros((LOCAL, CELLS), BF16)
+
+    @pl.when(g == GRP - 1)
+    def _():
+        turned[XB + 1] = jnp.zeros((LOCAL, CELLS), BF16)
 
     own = v * LOCAL + lax.broadcasted_iota(jnp.int32, (LOCAL, PZ), 0)
     ux, uy, uz = velocities(own)
@@ -186,13 +195,11 @@
             value = rest * block + rate_x * along_x + rate_y * along_y + rate_z * along_z
             store(pl.ds((base_block + j) * PZ, PZ), value.astype(BF16))
 
-    def target(k):
-        o = (k * STEP) & (VEL - 1)
-        da, db, dc = (o >> 1) & 3, o >> 3, o & 1
-        dx = jnp.where(core == 0, da, db)
-        dy = jnp.where(core == 0, db, da)
-        y, x = v >> 3, (v >> 1) & 3
-        return (((y + dy) & 3) << 3) + (((x + dx) & 3) << 1) + ((core + dc) & 1)
+    def chip(k):
+        word = jnp.where(k < 7, PACKED[0], jnp.where(k < 14, PACKED[1], PACKED[2]))
+        code = (word >> (4 * lax.rem(k, 7))) & 15
+        da, db = code & 3, code >> 2
+        return jnp.where(core == 0, da, db), jnp.where(core == 0, db, da)
 
     own_rows = pl.ds(pl.multiple_of(v * LOCAL, LOCAL), LOCAL)
 
@@ -208,40 +215,68 @@
             device_id={"vel": layer}, device_id_type=MESH,
         ).start()
 
-    for c in range(CHUNKS):
-
-        def step(k, _):
-            layer = target(k)
-            if c < EARLY:
-
-                @pl.when((layer > 0) & (layer < XB - 1))
-                def _():
+    def to_sibling(c, inner):
+        layer = v ^ 1
+        if inner:
+
+            @pl.when((layer > 0) & (layer < XB - 1))
+            def _():
+                advect_and_send(layer, c)
+        else:
+            advect_and_send(layer, c)
+
+    def to_chips(span, c, inner=False, back=False):
+        def step(i, _):
+            dx, dy = chip(span[0] + span[1] - 1 - i if back else i)
+            for dc in (0, 1):
+                layer = device(dx, dy, dc)
+                if inner:
+
+                    @pl.when((layer > 0) & (layer < XB - 1))
+                    def _():
+                        advect_and_send(layer, c)
+                else:
                     advect_and_send(layer, c)
-            else:
+            return 0
+
+        lax.fori_loop(span[0], span[1], step, 0)
+
+    ahead = 3
+    for c in range(ahead):
+        to_sibling(c, True)
+        to_chips(ONE, c, True)
+    hear(0)
+    tell(1)
+
+    @pl.when(g > 0)
+    def _():
+        to_upper().wait_recv()
+
+    @pl.when(g < GRP - 1)
+    def _():
+        to_lower().wait_recv()
+
+    for layer in (0, XB - 1):
+        far_x = ((v >> 1) - (layer >> 1)) & 3
+        far_y = ((v >> 3) - (layer >> 3)) & 3
+        far = jnp.minimum(far_x, 4 - far_x) + jnp.minimum(far_y, 4 - far_y)
+
+        @pl.when((far <= 1) & (v != layer))
+        def _():
+            for c in range(ahead):
                 advect_and_send(layer, c)
-            return 0
-
-        lax.fori_loop(1, VEL, step, 0)
-        if c == 0:
-            for i in range(FIRST, len(PIECES)):
-                turn(i)
-            send_ends()
-        if c == EARLY - 1:
-
-            @pl.when(g > 0)
-            def _():
-                to_upper().wait_recv()
-
-            @pl.when(g < GRP - 1)
-            def _():
-                to_lower().wait_recv()
-
-            for layer in (0, XB - 1):
-
-                @pl.when(v != layer)
-                def _():
-                    for early in range(EARLY):
-                        advect_and_send(layer, early)
+
+    to_chips(TWO, 0)
+    hear(1)
+    tell(2)
+    to_chips(TWO, 1)
+    to_chips(THREE, 0)
+    hear(2)
+    to_chips(FOUR, 0)
+    to_chips((THREE[0], FOUR[1]), 1)
+    to_chips((TWO[0], FOUR[1]), 2)
+    to_chips((ONE[0], FOUR[1]), 3, back=True)
+    to_sibling(3, False)
 
     def store_own(at, value):
         mu[own_rows, at] = value
@@ -308,15 +343,20 @@
             for i in range(VEL):
                 part[i] = total[i : i + 1]
 
-            def give(k, _):
-                owner = target(k)
+            def give(owner):
                 pltpu.make_async_remote_copy(
                     src_ref=part.at[owner], dst_ref=part_in.at[v], send_sem=psend_sem, recv_sem=precv_sem,
                     device_id={"vel": owner}, device_id_type=MESH,
                 ).start()
+
+            def give_chip(i, _):
+                dx, dy = chip(len(CHIPS) - 1 - i)
+                for dc in (0, 1):
+                    give(device(dx, dy, dc))
                 return 0
 
-            lax.fori_loop(1, VEL, give, 0)
+            lax.fori_loop(0, len(CHIPS), give_chip, 0)
+            give(v ^ 1)
 
         moments = (fluid * relax_c) * ((first - wall * second) / total_weight)
         high, low = split(moments)
@@ -402,6 +442,7 @@
             pltpu.VMEM((VEL, 1, 128), F32),
             pltpu.VMEM((VEL, 1, 128), F32),
             pltpu.VMEM((VEL, 128), F32),
+            pltpu.SemaphoreType.REGULAR((3,)),
             dma((len(PIECES),)),
             dma((5,)),
             dma((2,)),

time: 41.8 us -> 41 us (0.981)
  Pallas kernels: 40.9 us -> 39.9 us
    pallas_call x1, Pallas kernels: 39.5 us -> 38.6 us  [body(): pl.pallas_call(kernel, out_shape=(pltpu.VMEM((Q, CELLS), BF16), pltpu.VME...]
where the time goes in v4:
time: 41 us; the launch traced here: 40.5 us
  Pallas kernels  39.9 us (97%)
  between operations  0.64 us (2%)
    pallas_call x1, Pallas kernels, body(): pl.pallas_call(kernel, out_shape=(pltpu.VMEM((Q, CELLS), BF16), pltpu.VME...  38.6 us
    pallas_call x1, Pallas kernels, body(): pl.pallas_call(store_kernel, out_shape=(jax.ShapeDtypeStruct((Q, CELLS),...  1.36 us

profile of v4, /device:TPU:1, one launch (start us, length us, event | category | flops | bytes accessed | tf_op | source)
XLA Modules:
  0.0 40.5 jit_solution(7441532230432632107)
XLA Ops:
  0.6 38.6 %adjoint_step.1 = (bf16[512,2048]{1,0:T(8,128)(2,1)S(1)}, f32[1,128]{1,0:T(1,128)S(1)}) custom-call(bf16[16,1,32,2048]{3,2,1,0:T(8,128)(2,1)} %adj_hbm.1, f32[1,1,2048]{2,1,0:T(1,128)} %relax_hbm.1, f32[1,1,2048]{2,1,0:T(1,128)} %react_hbm.1, f32[10,1,1,2048]{3,2,1,0:T(1,128)} %base_hbm.1, s32[1,1,2048]{2,1,0:T(1,128)} %kind_hbm.1, s32[1,1,2048]{2,1,0:T(1,128)} %patch_hbm.1), custom_call_target="tpu_custom_call" | custom-call | tf_op jit(solution)/shard_map/adjoint_step/pallas_call | solution.py:424
  39.2 1.4 %store_step.1 = (bf16[512,2048]{1,0:T(8,128)(2,1)}, f32[1,16]{1,0:T(1,128)}) custom-call(bf16[512,2048]{1,0:T(8,128)(2,1)S(1)} %get-tuple-element.6.result, f32[1,128]{1,0:T(1,128)S(1)} %get-tuple-element.7.grad), custom_call_target="tpu_custom_call" | custom-call | tf_op jit(solution)/shard_map/store_step/pallas_call | solution.py:460

commit v5 on v2

--- a/solution.py
+++ b/solution.py
@@ -20,8 +20,13 @@
 LOCAL = Q // VEL
 CHUNKS = 4
 WIDTH = CELLS // CHUNKS
+BLOCKS = WIDTH // PZ
+PAIRS = ((6, 14), (9, 11), (5, 15), (13, 7), (2, 8), (1, 3), (4, 12))
+FARTHEST = 10
+PACKED = tuple(sum(pair[member] << (4 * i) for i, pair in enumerate(PAIRS)) for member in (0, 1))
 ROWS = 128
-STEP = 13
+TABLE = 32
+STORES = 4
 
 MESH = pl.DeviceIdType.MESH
 F32 = jnp.float32
@@ -77,8 +82,14 @@
     g = lax.axis_index("grp")
     core = v & 1
 
-    load = pltpu.make_async_copy(adj_hbm.at[:, 0], xin, load_sem)
-    load.start()
+    def chunk(c):
+        return pl.ds(c * WIDTH, WIDTH) if isinstance(c, int) else pl.ds(pl.multiple_of(c * WIDTH, WIDTH), WIDTH)
+
+    def load(i):
+        return pltpu.make_async_copy(adj_hbm.at[:, 0, :, chunk(i)], xin.at[:, :, chunk(i)], load_sem.at[i])
+
+    for i in range(CHUNKS):
+        load(i).start()
     smalls = [
         pltpu.make_async_copy(relax_hbm.at[0], relax, small_sem.at[0]),
         pltpu.make_async_copy(react_hbm.at[0], react, small_sem.at[1]),
@@ -89,6 +100,10 @@
     for copy in smalls:
         copy.start()
 
+    def device(dx, dy, dc):
+        y, x = v >> 3, (v >> 1) & 3
+        return (((y + dy) & 3) << 3) + (((x + dx) & 3) << 1) + ((core + dc) & 1)
+
     barrier = pltpu.get_barrier_semaphore()
 
     def greet(k, _):
@@ -105,16 +120,11 @@
     def _():
         pl.semaphore_signal(barrier, inc=1, device_id={"grp": g + 1}, device_id_type=MESH)
 
-    row = lax.broadcasted_iota(jnp.int32, (256, 256), 0)
-    col = lax.broadcasted_iota(jnp.int32, (256, 256), 1)
-    perm = jnp.where(col == ((row & 15) << 4) + (row >> 4), 1.0, 0.0).astype(BF16)
-    load.wait()
-    for t in range(2):
-        for c in range(CHUNKS):
-            cols = pl.ds(c * WIDTH, WIDTH)
-            block = xin[:, pl.ds(16 * t, 16), cols].reshape(256, WIDTH)
-            moved = jnp.dot(perm, block, preferred_element_type=F32).astype(BF16)
-            turned[pl.ds(1 + 16 * t, 16), :, cols] = moved.reshape(16, LOCAL, WIDTH)
+    for i in range(CHUNKS):
+        load(i).wait()
+        for t in range(XB // 16):
+            block = xin[:, pl.ds(16 * t, 16), chunk(i)]
+            turned[pl.ds(1 + 16 * t, 16), :, chunk(i)] = jnp.swapaxes(block, 0, 1)
 
     neighbours = jnp.where(g > 0, 1, 0) + jnp.where(g < GRP - 1, 1, 0)
     pl.semaphore_wait(barrier, VEL - 1 + neighbours)
@@ -156,32 +166,40 @@
     shift_z = jnp.where(((v >> 2) & 1) == 1, PZ - 1, 1)
 
     def advect(layer, c, store):
-        count = WIDTH // PZ
+        base_block = c * BLOCKS
 
         def cells(at, j):
             return turned[at, :, pl.ds((j % PY) * PZ, PZ)].astype(F32)
 
-        centre = [cells(layer + 1, c * count + j) for j in range(-1, count + 1)]
-        for j in range(count):
+        centre = [cells(layer + 1, base_block + j) for j in range(-1, BLOCKS + 1)]
+        for j in range(BLOCKS):
             block = centre[j + 1]
-            along_x = jnp.where(forward_x, cells(layer + 2, c * count + j), cells(layer, c * count + j))
+            along_x = jnp.where(forward_x, cells(layer + 2, base_block + j), cells(layer, base_block + j))
             along_y = jnp.concatenate([centre[j][:half], centre[j + 2][half:]], axis=0)
             along_z = pltpu.roll(block, shift_z, 1)
             value = rest * block + rate_x * along_x + rate_y * along_y + rate_z * along_z
-            store(pl.ds((c * count + j) * PZ, PZ), value.astype(BF16))
-
-    def target(k):
-        o = (k * STEP) & (VEL - 1)
-        da, db, dc = (o >> 1) & 3, o >> 3, o & 1
-        dx = jnp.where(core == 0, da, db)
-        dy = jnp.where(core == 0, db, da)
-        y, x = v >> 3, (v >> 1) & 3
-        return (((y + dy) & 3) << 3) + (((x + dx) & 3) << 1) + ((core + dc) & 1)
+            store(pl.ds((base_block + j) * PZ, PZ), value.astype(BF16))
+
+    def each(send):
+        def both(codes):
+            for dc in (0, 1):
+                for code in codes:
+                    da, db = code & 3, code >> 2
+                    dx, dy = jnp.where(core == 0, da, db), jnp.where(core == 0, db, da)
+                    send(device(dx, dy, dc))
+
+        def pair(i, _):
+            both([(word >> (4 * i)) & 15 for word in PACKED])
+            return 0
+
+        both([FARTHEST])
+        lax.fori_loop(0, len(PAIRS), pair, 0)
+        send(v ^ 1)
 
     own_rows = pl.ds(pl.multiple_of(v * LOCAL, LOCAL), LOCAL)
 
     def advect_and_send(layer, c):
-        cols = pl.ds(c * WIDTH, WIDTH)
+        cols = chunk(c)
 
         def store(at, value):
             staged[layer, :, at] = value
@@ -194,8 +212,7 @@
 
     for c in range(CHUNKS):
 
-        def step(k, _):
-            layer = target(k)
+        def send(layer):
             if c == 0:
 
                 @pl.when((layer > 0) & (layer < XB - 1))
@@ -203,9 +220,8 @@
                     advect_and_send(layer, c)
             else:
                 advect_and_send(layer, c)
-            return 0
-
-        lax.fori_loop(1, VEL, step, 0)
+
+        each(send)
         if c == 0:
 
             @pl.when(g > 0)
@@ -228,32 +244,37 @@
     for c in range(CHUNKS):
         advect(v, c, store_own)
 
-    q_row = lax.broadcasted_iota(jnp.int32, (64, Q), 1)
-    j_row = lax.broadcasted_iota(jnp.int32, (64, Q), 0)
-    ux, uy, uz = velocities(q_row)
-    speed = ux * ux + uy * uy + uz * uz
-    weight = jnp.exp(-speed)
-    total_weight = jnp.sum(weight[0:8], axis=1, keepdims=True)[0:1]
-    entry = poly(j_row & 15, ux, uy, uz) * jnp.where((j_row & 16) == 0, weight, weight * (speed / 3.0))
-    high = entry.astype(BF16).astype(F32)
-    etab[...] = jnp.where(j_row < 32, high, entry - high).astype(BF16)
-
-    for r in range(Q // ROWS):
-        rows = pl.ds(r * ROWS, ROWS)
-        q_col = r * ROWS + lax.broadcasted_iota(jnp.int32, (ROWS, 128), 0)
-        j_col = lax.broadcasted_iota(jnp.int32, (ROWS, 128), 1)
-        ux, uy, uz = velocities(q_col)
+    def columns(i, whole):
+        at = pl.ds(pl.multiple_of(i * 128, 128), 128)
+        ux, uy, uz = velocities(i * 128 + lax.broadcasted_iota(jnp.int32, (64, 128), 1))
+        j = lax.broadcasted_iota(jnp.int32, (64, 128), 0)
+        speed = ux * ux + uy * uy + uz * uz
+        weight = jnp.exp(-speed)
+        entry = poly(j & 15, ux, uy, uz) * jnp.where((j & 16) == 0, weight, weight * (speed / 3.0))
+        high = entry.astype(BF16).astype(F32)
+        etab[:, at] = jnp.where(j < 32, high, entry - high).astype(BF16)
+        return whole + jnp.sum(weight[0:8], axis=1, keepdims=True)[0:1]
+
+    total_weight = lax.fori_loop(0, Q // 128, columns, jnp.zeros((1, 1), F32))
+
+    def fill(r, _):
+        rows = pl.ds(pl.multiple_of(r * TABLE, TABLE), TABLE)
+        ux, uy, uz = velocities(r * TABLE + lax.broadcasted_iota(jnp.int32, (TABLE, 128), 0))
+        j = lax.broadcasted_iota(jnp.int32, (TABLE, 128), 1)
         absorb_tab[rows, :] = (ux * ux + uy * uy + uz * uz) / 3.0
-        entry = poly(j_col & 15, ux, uy, uz)
+        entry = poly(j & 15, ux, uy, uz)
         high = entry.astype(BF16).astype(F32)
-        btab[rows, :] = jnp.where((j_col & 16) == 0, high, entry - high).astype(BF16)
+        btab[rows, :] = jnp.where((j & 16) == 0, high, entry - high).astype(BF16)
+        return 0
+
+    lax.fori_loop(0, Q // TABLE, fill, 0)
 
     for copy in smalls:
         copy.wait()
 
     total[...] = jnp.zeros((VEL, 128), F32)
-    for c in range(CHUNKS):
-        cols = pl.ds(c * WIDTH, WIDTH)
+    def collide(c, _):
+        cols = chunk(c)
         arrived = mu.at[pl.ds(0, (VEL - 1) * LOCAL), cols]
         pltpu.make_async_copy(arrived, arrived, recv_sem.at[c]).wait()
         product = jnp.dot(etab[...], mu[:, cols], preferred_element_type=F32)
@@ -283,34 +304,39 @@
             preferred_element_type=F32,
         )
         total[...] += sums[0:VEL] + sums[VEL : 2 * VEL] + sums[2 * VEL :]
-        if c == CHUNKS - 1:
+        @pl.when(c == CHUNKS - 1)
+        def _():
             for i in range(VEL):
                 part[i] = total[i : i + 1]
 
-            def give(k, _):
-                owner = target(k)
+            def give(owner):
                 pltpu.make_async_remote_copy(
                     src_ref=part.at[owner], dst_ref=part_in.at[v], send_sem=psend_sem, recv_sem=precv_sem,
                     device_id={"vel": owner}, device_id_type=MESH,
                 ).start()
-                return 0
-
-            lax.fori_loop(1, VEL, give, 0)
+
+            each(give)
 
         moments = (fluid * relax_c) * ((first - wall * second) / total_weight)
         high, low = split(moments)
         stacked = jnp.concatenate([high, high, low, low], axis=0)
         keep = fluid * (1.0 - relax_c)
         keep_wall = keep * wall
-        for r in range(Q // ROWS):
-            rows = pl.ds(r * ROWS, ROWS)
+        def rows_of(r, _):
+            rows = pl.ds(pl.multiple_of(r * ROWS, ROWS), ROWS)
             collided = jnp.dot(btab[rows, 0:64], stacked, preferred_element_type=F32)
             for j in range(WIDTH // 128):
                 sub = slice(j * 128, (j + 1) * 128)
-                at = pl.ds(c * WIDTH + j * 128, 128)
+                at = pl.ds(pl.multiple_of(c * WIDTH + j * 128, 128), 128)
                 factor = keep[:, sub] - keep_wall[:, sub] * absorb_tab[rows, :]
                 value = factor * mu[rows, at].astype(F32) + collided[:, sub]
                 result[rows, at] = value.astype(BF16)
+            return 0
+
+        lax.fori_loop(0, Q // ROWS, rows_of, 0)
+        return 0
+
+    lax.fori_loop(0, CHUNKS, collide, 0)
 
     part_in[pl.ds(v, 1)] = part[pl.ds(v, 1)]
     sent = part.at[pl.ds(0, VEL - 1)]
@@ -335,8 +361,8 @@
 
 def store_kernel(result, grad, out_hbm, grad_hbm, small, out_sem, grad_sem):
     copies = []
-    for c in range(CHUNKS):
-        rows = pl.ds(c * (Q // CHUNKS), Q // CHUNKS)
+    for c in range(STORES):
+        rows = pl.ds(c * (Q // STORES), Q // STORES)
         copies.append(pltpu.make_async_copy(result.at[rows], out_hbm.at[rows], out_sem.at[c]))
     for copy in copies:
         copy.start()
@@ -381,7 +407,7 @@
             pltpu.VMEM((VEL, 1, 128), F32),
             pltpu.VMEM((VEL, 1, 128), F32),
             pltpu.VMEM((VEL, 128), F32),
-            dma,
+            dma((CHUNKS,)),
             dma((5,)),
             dma((2,)),
             dma((2,)),
@@ -400,7 +426,7 @@
         out_shape=(jax.ShapeDtypeStruct((Q, CELLS), BF16), jax.ShapeDtypeStruct((1, PATCH_DEV), F32)),
         in_specs=[vmem] * 2,
         out_specs=(hbm, hbm),
-        scratch_shapes=[pltpu.VMEM((1, PATCH_DEV), F32), dma((CHUNKS,)), dma],
+        scratch_shapes=[pltpu.VMEM((1, PATCH_DEV), F32), dma((STORES,)), dma],
         compiler_params=pltpu.CompilerParams(vmem_limit_bytes=8 * 1024 * 1024),
         name="store_step",
     )(in_vmem(result), in_vmem(grad))

time: 40.6 us -> 41 us (level)
  no operation moved by 1% of the time
where the time goes in v5:
time: 41 us; the launch traced here: 40.9 us
  Pallas kernels  40.3 us (98%)
  between operations  0.64 us (2%)
    pallas_call x1, Pallas kernels, body(): pl.pallas_call(kernel, out_shape=(pltpu.VMEM((Q, CELLS), BF16), pltpu.VME...  38.9 us
    pallas_call x1, Pallas kernels, body(): pl.pallas_call(store_kernel, out_shape=(jax.ShapeDtypeStruct((Q, CELLS),...  1.36 us

profile of v5, /device:TPU:1, one launch (start us, length us, event | category | flops | bytes accessed | tf_op | source)
XLA Modules:
  0.0 40.9 jit_solution(8193438652087892020)
XLA Ops:
  0.6 38.9 %adjoint_step.1 = (bf16[512,2048]{1,0:T(8,128)(2,1)S(1)}, f32[1,128]{1,0:T(1,128)S(1)}) custom-call(bf16[16,1,32,2048]{3,2,1,0:T(8,128)(2,1)} %adj_hbm.1, f32[1,1,2048]{2,1,0:T(1,128)} %relax_hbm.1, f32[1,1,2048]{2,1,0:T(1,128)} %react_hbm.1, f32[10,1,1,2048]{3,2,1,0:T(1,128)} %base_hbm.1, s32[1,1,2048]{2,1,0:T(1,128)} %kind_hbm.1, s32[1,1,2048]{2,1,0:T(1,128)} %patch_hbm.1), custom_call_target="tpu_custom_call" | custom-call | tf_op jit(solution)/shard_map/adjoint_step/pallas_call | solution.py:389
  39.5 1.4 %store_step.1 = (bf16[512,2048]{1,0:T(8,128)(2,1)}, f32[1,16]{1,0:T(1,128)}) custom-call(bf16[512,2048]{1,0:T(8,128)(2,1)S(1)} %get-tuple-element.6.result, f32[1,128]{1,0:T(1,128)S(1)} %get-tuple-element.7.grad), custom_call_target="tpu_custom_call" | custom-call | tf_op jit(solution)/shard_map/store_step/pallas_call | solution.py:424

commit v6 on v5

--- a/solution.py
+++ b/solution.py
@@ -20,9 +20,14 @@
 LOCAL = Q // VEL
 CHUNKS = 4
 WIDTH = CELLS // CHUNKS
-BLOCKS = WIDTH // PZ
+STARTS = (0, 512, 1024, 1536, 1664)
+SIZES = (512, 512, 512, 128, 384)
+LAST = len(SIZES) - 1
+GROUPS = SIZES[LAST] // PZ
+SUMS = 5
 PAIRS = ((6, 14), (9, 11), (5, 15), (13, 7), (2, 8), (1, 3), (4, 12))
 FARTHEST = 10
+NEAR = 2
 PACKED = tuple(sum(pair[member] << (4 * i) for i, pair in enumerate(PAIRS)) for member in (0, 1))
 ROWS = 128
 TABLE = 32
@@ -75,8 +80,8 @@
     adj_hbm, relax_hbm, react_hbm, base_hbm, kind_hbm, patch_hbm,
     result, grad_out,
     xin, turned, staged, mu, relax, react, base, kind, patch,
-    absorb_tab, etab, btab, part, part_in, total,
-    load_sem, small_sem, halo_send, halo_recv, send_sem, recv_sem, psend_sem, precv_sem,
+    absorb_tab, etab, btab, part, part_in, total, sums_out, sums_in, back,
+    round_sem, sums_sem, load_sem, small_sem, halo_send, halo_recv, send_sem, recv_sem, psend_sem, precv_sem,
 ):
     v = lax.axis_index("vel")
     g = lax.axis_index("grp")
@@ -84,6 +89,9 @@
 
     def chunk(c):
         return pl.ds(c * WIDTH, WIDTH) if isinstance(c, int) else pl.ds(pl.multiple_of(c * WIDTH, WIDTH), WIDTH)
+
+    def part_of(c):
+        return pl.ds(STARTS[c], SIZES[c])
 
     def load(i):
         return pltpu.make_async_copy(adj_hbm.at[:, 0, :, chunk(i)], xin.at[:, :, chunk(i)], load_sem.at[i])
@@ -105,12 +113,11 @@
         return (((y + dy) & 3) << 3) + (((x + dx) & 3) << 1) + ((core + dc) & 1)
 
     barrier = pltpu.get_barrier_semaphore()
-
-    def greet(k, _):
-        pl.semaphore_signal(barrier, inc=1, device_id={"vel": (v + k) & (VEL - 1)}, device_id_type=MESH)
-        return 0
-
-    lax.fori_loop(1, VEL, greet, 0)
+    pl.semaphore_signal(barrier, inc=1, device_id={"vel": v ^ 1}, device_id_type=MESH)
+    for code in sum(PAIRS[NEAR:], ()):
+        for dc in (0, 1):
+            near = device(code & 3, code >> 2, dc)
+            pl.semaphore_signal(barrier, inc=1, device_id={"vel": near}, device_id_type=MESH)
 
     @pl.when(g > 0)
     def _():
@@ -127,7 +134,9 @@
             turned[pl.ds(1 + 16 * t, 16), :, chunk(i)] = jnp.swapaxes(block, 0, 1)
 
     neighbours = jnp.where(g > 0, 1, 0) + jnp.where(g < GRP - 1, 1, 0)
-    pl.semaphore_wait(barrier, VEL - 1 + neighbours)
+    pl.semaphore_wait(barrier, 1 + 4 * (len(PAIRS) - NEAR) + neighbours)
+    for dx, dy in ((2, 0), (0, 2)):
+        pl.semaphore_signal(round_sem, inc=1, device_id={"vel": device(dx, dy, 0)}, device_id_type=MESH)
 
     def to_lower():
         return pltpu.make_async_remote_copy(
@@ -166,13 +175,13 @@
     shift_z = jnp.where(((v >> 2) & 1) == 1, PZ - 1, 1)
 
     def advect(layer, c, store):
-        base_block = c * BLOCKS
+        base_block, count = STARTS[c] // PZ, SIZES[c] // PZ
 
         def cells(at, j):
             return turned[at, :, pl.ds((j % PY) * PZ, PZ)].astype(F32)
 
-        centre = [cells(layer + 1, base_block + j) for j in range(-1, BLOCKS + 1)]
-        for j in range(BLOCKS):
+        centre = [cells(layer + 1, base_block + j) for j in range(-1, count + 1)]
+        for j in range(count):
             block = centre[j + 1]
             along_x = jnp.where(forward_x, cells(layer + 2, base_block + j), cells(layer, base_block + j))
             along_y = jnp.concatenate([centre[j][:half], centre[j + 2][half:]], axis=0)
@@ -180,68 +189,112 @@
             value = rest * block + rate_x * along_x + rate_y * along_y + rate_z * along_z
             store(pl.ds((base_block + j) * PZ, PZ), value.astype(BF16))
 
+    def both(codes, send):
+        for dc in (0, 1):
+            for code in codes:
+                da, db = code & 3, code >> 2
+                dx, dy = jnp.where(core == 0, da, db), jnp.where(core == 0, db, da)
+                send(device(dx, dy, dc))
+
+    def pairs(first, last, send):
+        def pair(i, _):
+            both([(word >> (4 * i)) & 15 for word in PACKED], send)
+            return 0
+
+        lax.fori_loop(first, last, pair, 0)
+
+    def far(send):
+        both([FARTHEST], send)
+        pairs(0, NEAR, send)
+
     def each(send):
-        def both(codes):
-            for dc in (0, 1):
-                for code in codes:
-                    da, db = code & 3, code >> 2
-                    dx, dy = jnp.where(core == 0, da, db), jnp.where(core == 0, db, da)
-                    send(device(dx, dy, dc))
-
-        def pair(i, _):
-            both([(word >> (4 * i)) & 15 for word in PACKED])
-            return 0
-
-        both([FARTHEST])
-        lax.fori_loop(0, len(PAIRS), pair, 0)
+        both([FARTHEST], send)
+        pairs(0, len(PAIRS), send)
         send(v ^ 1)
 
     own_rows = pl.ds(pl.multiple_of(v * LOCAL, LOCAL), LOCAL)
 
-    def advect_and_send(layer, c):
-        cols = chunk(c)
-
+    def advect_here(layer, c):
         def store(at, value):
             staged[layer, :, at] = value
 
         advect(layer, c, store)
+
+    def send_part(layer, c):
         pltpu.make_async_remote_copy(
-            src_ref=staged.at[layer, :, cols], dst_ref=mu.at[own_rows, cols], send_sem=send_sem, recv_sem=recv_sem.at[c],
-            device_id={"vel": layer}, device_id_type=MESH,
+            src_ref=staged.at[layer, :, part_of(c)], dst_ref=mu.at[own_rows, part_of(c)],
+            send_sem=send_sem, recv_sem=recv_sem.at[c], device_id={"vel": layer}, device_id_type=MESH,
         ).start()
 
-    for c in range(CHUNKS):
-
-        def send(layer):
-            if c == 0:
-
-                @pl.when((layer > 0) & (layer < XB - 1))
-                def _():
-                    advect_and_send(layer, c)
-            else:
-                advect_and_send(layer, c)
-
-        each(send)
-        if c == 0:
-
-            @pl.when(g > 0)
-            def _():
-                to_upper().wait_recv()
-
-            @pl.when(g < GRP - 1)
-            def _():
-                to_lower().wait_recv()
-
-            for layer in (0, XB - 1):
-
-                @pl.when(v != layer)
-                def _():
-                    advect_and_send(layer, 0)
+    def advect_and_send(layer, c):
+        advect_here(layer, c)
+        send_part(layer, c)
+
+    def inner(layer):
+        @pl.when((layer > 0) & (layer < XB - 1))
+        def _():
+            advect_and_send(layer, 0)
+
+    pairs(NEAR, len(PAIRS), inner)
+    inner(v ^ 1)
+    pl.semaphore_wait(round_sem, 2)
+    far(inner)
+
+    @pl.when(g > 0)
+    def _():
+        to_upper().wait_recv()
+
+    @pl.when(g < GRP - 1)
+    def _():
+        to_lower().wait_recv()
+
+    for layer in (0, XB - 1):
+
+        @pl.when(v != layer)
+        def _():
+            advect_and_send(layer, 0)
+
+    for c in range(1, LAST):
+        each(lambda layer: advect_and_send(layer, c))
+
+    lax.fori_loop(0, XB, lambda layer, _: (advect_here(layer, LAST), 0)[1], 0)
+    r_at = lax.broadcasted_iota(jnp.int32, (LOCAL, 256), 0)
+    q_at = lax.broadcasted_iota(jnp.int32, (LOCAL, 256), 1)
+    ux, uy, uz = velocities(v * LOCAL + (q_at & 15))
+    speed = ux * ux + uy * uy + uz * uz
+    weight = jnp.exp(-speed) * (speed / 3.0)
+    signed = jnp.where(uy > 0, weight, -weight)
+    factors = (weight, weight * ux, weight * ux * ux, signed, signed * ux)
+    same = (lax.broadcasted_iota(jnp.int32, (256, 256), 0) >> 4) == (lax.broadcasted_iota(jnp.int32, (256, 256), 1) >> 4)
+    tables = []
+    for j in range(GROUPS):
+        entry = jnp.zeros((LOCAL, 256), F32)
+        for i, factor in enumerate(factors):
+            entry = jnp.where(r_at == SUMS * j + i, factor, entry)
+        for piece in split(entry):
+            whole = jnp.concatenate([piece.astype(F32)] * 16, axis=0)
+            tables.append((j, jnp.where(same, whole, 0.0).astype(BF16)))
+    for t in range(XB // 16):
+        acc = jnp.zeros((256, PZ), F32)
+        for j, table in tables:
+            block = staged[pl.ds(16 * t, 16), :, pl.ds(STARTS[LAST] + j * PZ, PZ)].reshape(256, PZ)
+            acc = acc + jnp.dot(table, block, preferred_element_type=F32)
+        sums_out[pl.ds(256 * t, 256), :] = acc.astype(BF16)
+
+    def send_sums(layer):
+        pltpu.make_async_remote_copy(
+            src_ref=sums_out.at[pl.ds(pl.multiple_of(layer * LOCAL, LOCAL), LOCAL)], dst_ref=sums_in.at[own_rows],
+            send_sem=sums_sem.at[0], recv_sem=sums_sem.at[1], device_id={"vel": layer}, device_id_type=MESH,
+        ).start()
+
+    each(send_sums)
+    sums_in[own_rows, :] = sums_out[own_rows, :]
+    each(lambda layer: send_part(layer, LAST))
 
     def store_own(at, value):
         mu[own_rows, at] = value
 
-    for c in range(CHUNKS):
+    for c in range(len(SIZES)):
         advect(v, c, store_own)
 
     def columns(i, whole):
@@ -269,26 +322,42 @@
 
     lax.fori_loop(0, Q // TABLE, fill, 0)
 
+    r_at = lax.broadcasted_iota(jnp.int32, (GROUPS * 16, Q), 0)
+    q_at = lax.broadcasted_iota(jnp.int32, (GROUPS * 16, Q), 1)
+    k_at, i_at = r_at & 15, (q_at & 15) - SUMS * (r_at >> 4)
+    third = 1.0 / 3.0
+    side = jnp.abs(component(((q_at >> 4) & 3) * 2))
+    uz = component(q_at >> 6)
+    entry = jnp.zeros((GROUPS * 16, Q), F32)
+    for k, i, value in (
+        (0, 0, 1.0), (1, 1, 1.0), (2, 3, side), (3, 0, uz), (4, 2, 1.0), (4, 0, -third), (5, 0, side * side - third),
+        (6, 0, uz * uz - third), (7, 4, side), (8, 1, uz), (9, 3, uz * side),
+    ):
+        entry = jnp.where((k_at == k) & (i_at == i), value, entry)
+    high, low = split(entry)
+    back[...] = jnp.concatenate([high, low], axis=0)
+
     for copy in smalls:
         copy.wait()
 
     total[...] = jnp.zeros((VEL, 128), F32)
-    def collide(c, _):
-        cols = chunk(c)
+
+    def arrive(c, cols):
         arrived = mu.at[pl.ds(0, (VEL - 1) * LOCAL), cols]
         pltpu.make_async_copy(arrived, arrived, recv_sem.at[c]).wait()
+
+    def project(cols):
         product = jnp.dot(etab[...], mu[:, cols], preferred_element_type=F32)
-        first = product[0:16] + product[32:48]
-        second = product[16:32] + product[48:64]
-        kind_c = kind[:, cols]
-        wall = jnp.where(kind_c == 2, react[:, cols], 0.0)
-        fluid = jnp.where(kind_c != 0, 1.0, 0.0)
-        relax_c = relax[:, cols]
-
+        return product[0:16] + product[32:48], product[16:32] + product[48:64]
+
+    def wall_of(cols):
+        return jnp.where(kind[:, cols] == 2, react[:, cols], 0.0)
+
+    def add_patches(cols, second):
         acc = base[0, :, cols] * second[0:1]
         for k in range(1, MOMENTS):
             acc = acc + base[k, :, cols] * second[k : k + 1]
-        sens = -wall * acc / total_weight
+        sens = -wall_of(cols) * acc / total_weight
         patch_c = patch[:, cols]
         owner = lax.broadcasted_iota(jnp.int32, (VEL, WIDTH), 0) == (patch_c >> 7)
         spread = jnp.where(owner, sens, 0.0)
@@ -304,24 +373,18 @@
             preferred_element_type=F32,
         )
         total[...] += sums[0:VEL] + sums[VEL : 2 * VEL] + sums[2 * VEL :]
-        @pl.when(c == CHUNKS - 1)
-        def _():
-            for i in range(VEL):
-                part[i] = total[i : i + 1]
-
-            def give(owner):
-                pltpu.make_async_remote_copy(
-                    src_ref=part.at[owner], dst_ref=part_in.at[v], send_sem=psend_sem, recv_sem=precv_sem,
-                    device_id={"vel": owner}, device_id_type=MESH,
-                ).start()
-
-            each(give)
-
+
+    def relax_cells(c, first, second):
+        cols = chunk(c)
+        wall = wall_of(cols)
+        fluid = jnp.where(kind[:, cols] != 0, 1.0, 0.0)
+        relax_c = relax[:, cols]
         moments = (fluid * relax_c) * ((first - wall * second) / total_weight)
         high, low = split(moments)
         stacked = jnp.concatenate([high, high, low, low], axis=0)
         keep = fluid * (1.0 - relax_c)
         keep_wall = keep * wall
+
         def rows_of(r, _):
             rows = pl.ds(pl.multiple_of(r * ROWS, ROWS), ROWS)
             collided = jnp.dot(btab[rows, 0:64], stacked, preferred_element_type=F32)
@@ -334,9 +397,46 @@
             return 0
 
         lax.fori_loop(0, Q // ROWS, rows_of, 0)
+
+    def step(c, _):
+        cols = chunk(c)
+
+        @pl.when(c < CHUNKS - 1)
+        def _():
+            arrive(c, cols)
+            first, second = project(cols)
+            add_patches(cols, second)
+            relax_cells(c, first, second)
+
+        @pl.when(c == CHUNKS - 1)
+        def _():
+            arrive(LAST - 1, part_of(LAST - 1))
+            _, second = project(part_of(LAST - 1))
+            came = sums_in.at[pl.ds(0, (VEL - 1) * LOCAL)]
+            pltpu.make_async_copy(came, came, sums_sem.at[1]).wait()
+            product = jnp.dot(back[...], sums_in[...], preferred_element_type=F32)
+            later = [
+                product[16 * j : 16 * (j + 1)] + product[16 * (GROUPS + j) : 16 * (GROUPS + j + 1)]
+                for j in range(GROUPS)
+            ]
+            add_patches(cols, jnp.concatenate([second] + later, axis=1))
+            for i in range(VEL):
+                part[i] = total[i : i + 1]
+
+            def give(owner):
+                pltpu.make_async_remote_copy(
+                    src_ref=part.at[owner], dst_ref=part_in.at[v], send_sem=psend_sem, recv_sem=precv_sem,
+                    device_id={"vel": owner}, device_id_type=MESH,
+                ).start()
+
+            each(give)
+            arrive(LAST, part_of(LAST))
+            first, second = project(cols)
+            relax_cells(c, first, second)
+
         return 0
 
-    lax.fori_loop(0, CHUNKS, collide, 0)
+    lax.fori_loop(0, CHUNKS, step, 0)
 
     part_in[pl.ds(v, 1)] = part[pl.ds(v, 1)]
     sent = part.at[pl.ds(0, VEL - 1)]
@@ -347,6 +447,8 @@
     grad_out[...] = grad
 
     pltpu.make_async_copy(sent, sent, psend_sem).wait()
+    gone = sums_out.at[pl.ds(0, (VEL - 1) * LOCAL)]
+    pltpu.make_async_copy(gone, gone, sums_sem.at[0]).wait()
     staged_out = staged.at[pl.ds(0, VEL - 1)]
     pltpu.make_async_copy(staged_out, staged_out, send_sem).wait()
 
@@ -407,12 +509,17 @@
             pltpu.VMEM((VEL, 1, 128), F32),
             pltpu.VMEM((VEL, 1, 128), F32),
             pltpu.VMEM((VEL, 128), F32),
+            pltpu.VMEM((Q, PZ), BF16),
+            pltpu.VMEM((Q, PZ), BF16),
+            pltpu.VMEM((2 * GROUPS * 16, Q), BF16),
+            pltpu.SemaphoreType.REGULAR,
+            dma((2,)),
             dma((CHUNKS,)),
             dma((5,)),
             dma((2,)),
             dma((2,)),
             dma,
-            dma((CHUNKS,)),
+            dma((len(SIZES),)),
             dma,
             dma,
         ],

time: 41 us -> 41.6 us (1.015)
  Pallas kernels: 40.3 us -> 40.9 us
    pallas_call x1, Pallas kernels: 38.9 us -> 39.5 us  [body(): pl.pallas_call(kernel, out_shape=(pltpu.VMEM((Q, CELLS), BF16), pltpu.VME...]
where the time goes in v6:
time: 41.6 us; the launch traced here: 41.5 us
  Pallas kernels  40.9 us (98%)
  between operations  0.64 us (2%)
    pallas_call x1, Pallas kernels, body(): pl.pallas_call(kernel, out_shape=(pltpu.VMEM((Q, CELLS), BF16), pltpu.VME...  39.5 us
    pallas_call x1, Pallas kernels, body(): pl.pallas_call(store_kernel, out_shape=(jax.ShapeDtypeStruct((Q, CELLS),...  1.36 us

profile of v6, /device:TPU:1, one launch (start us, length us, event | category | flops | bytes accessed | tf_op | source)
XLA Modules:
  0.0 41.5 jit_solution(11502573390068938583)
XLA Ops:
  0.6 39.5 %adjoint_step.1 = (bf16[512,2048]{1,0:T(8,128)(2,1)S(1)}, f32[1,128]{1,0:T(1,128)S(1)}) custom-call(bf16[16,1,32,2048]{3,2,1,0:T(8,128)(2,1)} %adj_hbm.1, f32[1,1,2048]{2,1,0:T(1,128)} %relax_hbm.1, f32[1,1,2048]{2,1,0:T(1,128)} %react_hbm.1, f32[10,1,1,2048]{3,2,1,0:T(1,128)} %base_hbm.1, s32[1,1,2048]{2,1,0:T(1,128)} %kind_hbm.1, s32[1,1,2048]{2,1,0:T(1,128)} %patch_hbm.1), custom_call_target="tpu_custom_call" | custom-call | tf_op jit(solution)/shard_map/adjoint_step/pallas_call | solution.py:491
  40.1 1.4 %store_step.1 = (bf16[512,2048]{1,0:T(8,128)(2,1)}, f32[1,16]{1,0:T(1,128)}) custom-call(bf16[512,2048]{1,0:T(8,128)(2,1)S(1)} %get-tuple-element.6.result, f32[1,128]{1,0:T(1,128)S(1)} %get-tuple-element.7.grad), custom_call_target="tpu_custom_call" | custom-call | tf_op jit(solution)/shard_map/store_step/pallas_call | solution.py:531

commit v7 on v5

--- a/solution.py
+++ b/solution.py
@@ -23,6 +23,8 @@
 BLOCKS = WIDTH // PZ
 PAIRS = ((6, 14), (9, 11), (5, 15), (13, 7), (2, 8), (1, 3), (4, 12))
 FARTHEST = 10
+NEAR = 2
+STRIDE = 13
 PACKED = tuple(sum(pair[member] << (4 * i) for i, pair in enumerate(PAIRS)) for member in (0, 1))
 ROWS = 128
 TABLE = 32
@@ -75,8 +77,8 @@
     adj_hbm, relax_hbm, react_hbm, base_hbm, kind_hbm, patch_hbm,
     result, grad_out,
     xin, turned, staged, mu, relax, react, base, kind, patch,
-    absorb_tab, etab, btab, part, part_in, total,
-    load_sem, small_sem, halo_send, halo_recv, send_sem, recv_sem, psend_sem, precv_sem,
+    absorb_tab, etab, btab, part, part_in, total, coef, slots,
+    round_sem, load_sem, small_sem, halo_send, halo_recv, send_sem, recv_sem, psend_sem, precv_sem,
 ):
     v = lax.axis_index("vel")
     g = lax.axis_index("grp")
@@ -105,12 +107,11 @@
         return (((y + dy) & 3) << 3) + (((x + dx) & 3) << 1) + ((core + dc) & 1)
 
     barrier = pltpu.get_barrier_semaphore()
-
-    def greet(k, _):
-        pl.semaphore_signal(barrier, inc=1, device_id={"vel": (v + k) & (VEL - 1)}, device_id_type=MESH)
-        return 0
-
-    lax.fori_loop(1, VEL, greet, 0)
+    pl.semaphore_signal(barrier, inc=1, device_id={"vel": v ^ 1}, device_id_type=MESH)
+    for code in sum(PAIRS[NEAR:], ()):
+        for dc in (0, 1):
+            near = device(code & 3, code >> 2, dc)
+            pl.semaphore_signal(barrier, inc=1, device_id={"vel": near}, device_id_type=MESH)
 
     @pl.when(g > 0)
     def _():
@@ -127,7 +128,9 @@
             turned[pl.ds(1 + 16 * t, 16), :, chunk(i)] = jnp.swapaxes(block, 0, 1)
 
     neighbours = jnp.where(g > 0, 1, 0) + jnp.where(g < GRP - 1, 1, 0)
-    pl.semaphore_wait(barrier, VEL - 1 + neighbours)
+    pl.semaphore_wait(barrier, 1 + 4 * (len(PAIRS) - NEAR) + neighbours)
+    for dx, dy in ((2, 0), (0, 2)):
+        pl.semaphore_signal(round_sem, inc=1, device_id={"vel": device(dx, dy, 0)}, device_id_type=MESH)
 
     def to_lower():
         return pltpu.make_async_remote_copy(
@@ -180,20 +183,27 @@
             value = rest * block + rate_x * along_x + rate_y * along_y + rate_z * along_z
             store(pl.ds((base_block + j) * PZ, PZ), value.astype(BF16))
 
+    def both(codes, send):
+        for dc in (0, 1):
+            for code in codes:
+                da, db = code & 3, code >> 2
+                dx, dy = jnp.where(core == 0, da, db), jnp.where(core == 0, db, da)
+                send(device(dx, dy, dc))
+
+    def pairs(first, last, send):
+        def pair(i, _):
+            both([(word >> (4 * i)) & 15 for word in PACKED], send)
+            return 0
+
+        lax.fori_loop(first, last, pair, 0)
+
+    def far(send):
+        both([FARTHEST], send)
+        pairs(0, NEAR, send)
+
     def each(send):
-        def both(codes):
-            for dc in (0, 1):
-                for code in codes:
-                    da, db = code & 3, code >> 2
-                    dx, dy = jnp.where(core == 0, da, db), jnp.where(core == 0, db, da)
-                    send(device(dx, dy, dc))
-
-        def pair(i, _):
-            both([(word >> (4 * i)) & 15 for word in PACKED])
-            return 0
-
-        both([FARTHEST])
-        lax.fori_loop(0, len(PAIRS), pair, 0)
+        both([FARTHEST], send)
+        pairs(0, len(PAIRS), send)
         send(v ^ 1)
 
     own_rows = pl.ds(pl.multiple_of(v * LOCAL, LOCAL), LOCAL)
@@ -210,33 +220,32 @@
             device_id={"vel": layer}, device_id_type=MESH,
         ).start()
 
-    for c in range(CHUNKS):
-
-        def send(layer):
-            if c == 0:
-
-                @pl.when((layer > 0) & (layer < XB - 1))
-                def _():
-                    advect_and_send(layer, c)
-            else:
-                advect_and_send(layer, c)
-
-        each(send)
-        if c == 0:
-
-            @pl.when(g > 0)
-            def _():
-                to_upper().wait_recv()
-
-            @pl.when(g < GRP - 1)
-            def _():
-                to_lower().wait_recv()
-
-            for layer in (0, XB - 1):
-
-                @pl.when(v != layer)
-                def _():
-                    advect_and_send(layer, 0)
+    def inner(layer):
+        @pl.when((layer > 0) & (layer < XB - 1))
+        def _():
+            advect_and_send(layer, 0)
+
+    pairs(NEAR, len(PAIRS), inner)
+    inner(v ^ 1)
+    pl.semaphore_wait(round_sem, 2)
+    far(inner)
+
+    @pl.when(g > 0)
+    def _():
+        to_upper().wait_recv()
+
+    @pl.when(g < GRP - 1)
+    def _():
+        to_lower().wait_recv()
+
+    for layer in (0, XB - 1):
+
+        @pl.when(v != layer)
+        def _():
+            advect_and_send(layer, 0)
+
+    for c in range(1, CHUNKS):
+        each(lambda layer: advect_and_send(layer, c))
 
     def store_own(at, value):
         mu[own_rows, at] = value
@@ -272,7 +281,16 @@
     for copy in smalls:
         copy.wait()
 
+    coef[...] = jnp.zeros((16, CELLS), F32)
+    scale = -jnp.where(kind[...] == 2, react[...], 0.0) / total_weight
+    for k in range(MOMENTS):
+        coef[k : k + 1, :] = scale * base[k]
+    for c in range(CHUNKS):
+        slot = lax.broadcasted_iota(jnp.int32, (128, WIDTH), 0) == (patch[:, chunk(c)] & 15)
+        slots[:, chunk(c)] = jnp.where(slot, 1.0, 0.0).astype(BF16)
+
     total[...] = jnp.zeros((VEL, 128), F32)
+
     def collide(c, _):
         cols = chunk(c)
         arrived = mu.at[pl.ds(0, (VEL - 1) * LOCAL), cols]
@@ -285,10 +303,7 @@
         fluid = jnp.where(kind_c != 0, 1.0, 0.0)
         relax_c = relax[:, cols]
 
-        acc = base[0, :, cols] * second[0:1]
-        for k in range(1, MOMENTS):
-            acc = acc + base[k, :, cols] * second[k : k + 1]
-        sens = -wall * acc / total_weight
+        sens = jnp.sum(coef[:, cols] * second, axis=0, keepdims=True)
         patch_c = patch[:, cols]
         owner = lax.broadcasted_iota(jnp.int32, (VEL, WIDTH), 0) == (patch_c >> 7)
         spread = jnp.where(owner, sens, 0.0)
@@ -296,16 +311,14 @@
         left = spread - piece0.astype(F32)
         piece1 = left.astype(BF16)
         piece2 = (left - piece1.astype(F32)).astype(BF16)
-        slot = lax.broadcasted_iota(jnp.int32, (128, WIDTH), 0) == (patch_c & 15)
         sums = lax.dot_general(
             jnp.concatenate([piece0, piece1, piece2], axis=0),
-            jnp.where(slot, 1.0, 0.0).astype(BF16),
+            slots[:, cols],
             (((1,), (1,)), ((), ())),
             preferred_element_type=F32,
         )
         total[...] += sums[0:VEL] + sums[VEL : 2 * VEL] + sums[2 * VEL :]
-        @pl.when(c == CHUNKS - 1)
-        def _():
+        if c == CHUNKS - 1:
             for i in range(VEL):
                 part[i] = total[i : i + 1]
 
@@ -315,7 +328,12 @@
                     device_id={"vel": owner}, device_id_type=MESH,
                 ).start()
 
-            each(give)
+            def give_next(k, _):
+                o = (k * STRIDE) & (VEL - 1)
+                give(device((o >> 1) & 3, o >> 3, o & 1))
+                return 0
+
+            lax.fori_loop(1, VEL, give_next, 0)
 
         moments = (fluid * relax_c) * ((first - wall * second) / total_weight)
         high, low = split(moments)
@@ -336,7 +354,8 @@
         lax.fori_loop(0, Q // ROWS, rows_of, 0)
         return 0
 
-    lax.fori_loop(0, CHUNKS, collide, 0)
+    for c in range(CHUNKS):
+        collide(c, 0)
 
     part_in[pl.ds(v, 1)] = part[pl.ds(v, 1)]
     sent = part.at[pl.ds(0, VEL - 1)]
@@ -407,6 +426,9 @@
             pltpu.VMEM((VEL, 1, 128), F32),
             pltpu.VMEM((VEL, 1, 128), F32),
             pltpu.VMEM((VEL, 128), F32),
+            pltpu.VMEM((16, CELLS), F32),
+            pltpu.VMEM((128, CELLS), BF16),
+            pltpu.SemaphoreType.REGULAR,
             dma((CHUNKS,)),
             dma((5,)),
             dma((2,)),

time: 41 us -> 40.7 us (level)
  no operation moved by 1% of the time
where the time goes in v7:
time: 40.7 us; the launch traced here: 40.6 us
  Pallas kernels  40 us (98%)
  between operations  0.64 us (2%)
    pallas_call x1, Pallas kernels, body(): pl.pallas_call(kernel, out_shape=(pltpu.VMEM((Q, CELLS), BF16), pltpu.VME...  38.6 us
    pallas_call x1, Pallas kernels, body(): pl.pallas_call(store_kernel, out_shape=(jax.ShapeDtypeStruct((Q, CELLS),...  1.36 us

profile of v7, /device:TPU:1, one launch (start us, length us, event | category | flops | bytes accessed | tf_op | source)
XLA Modules:
  0.0 40.6 jit_solution(5200663852543090179)
XLA Ops:
  0.6 38.6 %adjoint_step.1 = (bf16[512,2048]{1,0:T(8,128)(2,1)S(1)}, f32[1,128]{1,0:T(1,128)S(1)}) custom-call(bf16[16,1,32,2048]{3,2,1,0:T(8,128)(2,1)} %adj_hbm.1, f32[1,1,2048]{2,1,0:T(1,128)} %relax_hbm.1, f32[1,1,2048]{2,1,0:T(1,128)} %react_hbm.1, f32[10,1,1,2048]{3,2,1,0:T(1,128)} %base_hbm.1, s32[1,1,2048]{2,1,0:T(1,128)} %kind_hbm.1, s32[1,1,2048]{2,1,0:T(1,128)} %patch_hbm.1), custom_call_target="tpu_custom_call" | custom-call | tf_op jit(solution)/shard_map/adjoint_step/pallas_call | solution.py:408
  39.2 1.4 %store_step.1 = (bf16[512,2048]{1,0:T(8,128)(2,1)}, f32[1,16]{1,0:T(1,128)}) custom-call(bf16[512,2048]{1,0:T(8,128)(2,1)S(1)} %get-tuple-element.6.result, f32[1,128]{1,0:T(1,128)S(1)} %get-tuple-element.7.grad), custom_call_target="tpu_custom_call" | custom-call | tf_op jit(solution)/shard_map/store_step/pallas_call | solution.py:446
